TPU v7x, 768 devices: a whole 4x8x12 slice. The times are simulated.
768 devices in a mesh: group: 24 (over z, x_lo), expert: 8 (over y), tensor: 4 (over x_hi, core).
Axes of the slice: x: 4 (x_hi: 2, x_lo: 2; x = x_hi * 2 + x_lo), y: 8, z: 12, core: 2. Of those that a mesh axis runs over, the one named last changes fastest.
Arguments:
- tokens: bfloat16 [4, 1536, 6144], P(None, ('group', 'expert')), may hold values from -6 to 6
- expert_ids: int32 [4, 1536, 2], P(None, ('group', 'expert')), may hold values from 0 to 7, all different within a row; in each aligned block of 8 rows (0 to 7, 8 to 15, ..., all dimensions but the last counted through in order) at most 4 rows name the same one
- gate_values: float32 [4, 1536, 2], P(None, ('group', 'expert')), may hold values from 0.2 to 1
- rollout_gate_up: bfloat16 [8, 2, 6144, 1024], P('expert', None, None, 'tensor'), may hold values from -0.078125 to 0.078125
- learner_gate_up: float32 [8, 2, 6144, 1024], P('expert', None, 'group', 'tensor'), may hold values from -0.688919 to 0.688919
- down_weight: bfloat16 [8, 1024, 6144], P('expert', 'tensor'), may hold values from -0.1875 to 0.1875
Outputs:
- mixed: bfloat16 [4, 1536, 6144], P(None, ('group', 'expert'), 'tensor')
Inputs may be any that keep to these rules, and one draw needn't show every extreme that they name: `expert_ids`: in each step the 8 tokens of one device (aligned blocks of 8 rows) name one expert at most 4 times, and some block reaches 4; the 2 experts of a token differ.
All inputs are finite; a program needn't handle non-finite values.
Results may differ from a plain program's by a relative error of at most 0.014.
Values may be sent and summed in bfloat16 or wider, within the bound.
No kernel may reach another device: no remote copies, remote signals or barrier semaphores. Data moves between devices by JAX's collectives and lax.ppermute only.
A program may use at most 128 MiB of HBM per device.

v0:
```python
import jax
import jax.numpy as jnp
from jax import lax
from jax.sharding import PartitionSpec as P

BLOCK = 128


clip_level = 2.0
epsilon = 1e-06


def block_scales(change):
    expert_count, pair_count, row_count, col_count = change.shape
    blocks = change.reshape(
        expert_count, pair_count, row_count // BLOCK, BLOCK, col_count // BLOCK, BLOCK
    )
    mean_square = jnp.mean(blocks * blocks, axis=(3, 5))
    return jnp.sqrt(mean_square + epsilon).astype(jnp.bfloat16)


def quantize(change, scales):
    expert_count, pair_count, row_count, col_count = change.shape
    blocks = change.reshape(
        expert_count, pair_count, row_count // BLOCK, BLOCK, col_count // BLOCK, BLOCK
    )
    expanded = scales.astype(jnp.float32)[:, :, :, None, :, None]
    levels = jnp.clip(blocks / expanded, -clip_level, clip_level)
    return levels.reshape(change.shape).astype(jnp.bfloat16)


def apply_levels(current, levels, per_row):
    expert_count, pair_count, row_count, col_count = current.shape
    expanded = levels.astype(jnp.float32).reshape(
        expert_count, pair_count, row_count, col_count // BLOCK, BLOCK
    )
    step_size = per_row.astype(jnp.float32)[..., None]
    added = (expanded * step_size).reshape(current.shape)
    return (current.astype(jnp.float32) + added).astype(jnp.bfloat16)


def slot_tables(step_ids, step_gates, expert_count, capacity):
    token_count, top_count = step_ids.shape
    flat_ids = step_ids.reshape(-1)
    one_hot = (flat_ids[:, None] == jnp.arange(expert_count, dtype=jnp.int32)[None, :]).astype(
        jnp.int32
    )
    earlier = jnp.cumsum(one_hot, axis=0) - one_hot
    slot_index = jnp.sum(earlier * one_hot, axis=1)
    position = (flat_ids * capacity + slot_index).reshape(token_count, top_count)
    slot_range = jnp.arange(expert_count * capacity, dtype=jnp.int32)
    matches = position[None, :, :] == slot_range[:, None, None]
    dispatch = jnp.any(matches, axis=2).astype(jnp.bfloat16)
    combine = jnp.sum(
        jnp.where(matches, step_gates[None, :, :], jnp.zeros_like(step_gates)[None, :, :]), axis=2
    ).T
    return (dispatch, combine)


def shards(tokens, expert_ids, gate_values, rollout_gate_up, learner_gate_up, down_weight):
    expert_count = lax.axis_size("expert")
    tensor_count = lax.axis_size("tensor")
    step_count, token_count, width = tokens.shape
    top_count = expert_ids.shape[2]
    capacity = min(token_count, 2 * token_count * top_count // expert_count)
    quarter = width // tensor_count
    own_rows = learner_gate_up.shape[2]
    slot_rows = expert_count * capacity
    row_start = lax.axis_index("group") * own_rows
    mine = lax.dynamic_slice_in_dim(rollout_gate_up, row_start, own_rows, 2)
    change = learner_gate_up - mine.astype(jnp.float32)
    scales = block_scales(change)
    levels = quantize(change, scales)
    per_row = jnp.repeat(scales, BLOCK, axis=2)
    piece_levels, piece_scales = lax.all_gather((levels, per_row), "group", axis=2, tiled=True)
    synced = apply_levels(rollout_gate_up, piece_levels, piece_scales)
    combines = []
    arrivals = []
    for step_index in range(step_count):
        dispatch, combine = slot_tables(
            expert_ids[step_index], gate_values[step_index], expert_count, capacity
        )
        combines.append(combine)
        outgoing = jnp.dot(dispatch, tokens[step_index], preferred_element_type=jnp.float32).astype(
            jnp.bfloat16
        )
        outgoing = outgoing.reshape(expert_count, capacity, width)
        arrived = lax.all_to_all(outgoing, "expert", split_axis=0, concat_axis=0, tiled=True)
        arrivals.append(arrived.reshape(slot_rows, width))
    received = jnp.concatenate(arrivals, axis=0)
    gate = jnp.dot(received, synced[0, 0], preferred_element_type=jnp.float32)
    upper = jnp.dot(received, synced[0, 1], preferred_element_type=jnp.float32)
    hidden = (jax.nn.silu(gate) * upper).astype(jnp.bfloat16)
    columns = down_weight[0]
    summed = lax.psum_scatter(
        lax.dot_general(
            columns, hidden, (((0,), (1,)), ((), ())), preferred_element_type=jnp.float32
        ).astype(jnp.bfloat16),
        "tensor",
        scatter_dimension=0,
        tiled=True,
    ).astype(jnp.float32)
    expert_all = summed.T.astype(jnp.bfloat16)
    outputs = []
    for step_index in range(step_count):
        expert_out = expert_all[step_index * slot_rows : (step_index + 1) * slot_rows].reshape(
            expert_count, capacity, quarter
        )
        back = lax.all_to_all(expert_out, "expert", split_axis=0, concat_axis=0, tiled=True)
        mixed = jnp.dot(
            combines[step_index],
            back.reshape(slot_rows, quarter).astype(jnp.float32),
            precision=lax.Precision.HIGHEST,
        )
        outputs.append(mixed.astype(jnp.bfloat16))
    return jnp.stack(outputs, axis=0)


def solution(mesh):
    in_specs = (
        P(None, ("group", "expert"), None),
        P(None, ("group", "expert"), None),
        P(None, ("group", "expert"), None),
        P("expert", None, None, "tensor"),
        P("expert", None, "group", "tensor"),
        P("expert", "tensor", None),
    )
    out_specs = P(None, ("group", "expert"), "tensor")
    return jax.shard_map(shards, mesh=mesh, in_specs=in_specs, out_specs=out_specs, check_vma=False)
```

profile of v0, /device:TPU:1, one launch (start us, length us, event | category | flops | bytes accessed | tf_op | source)
XLA Modules:
  0.0 450.7 jit_solution(10342841611920044453)
XLA Ops:
  6.5 2.1 fusion.10
  8.7 2.1 mul.82
  13.7 2.2 div.23
  15.9 2.1 clamp_convert_fusion
  21.9 7.7 %all-to-all-start = ((bf16[8,4,6144]{2,1,0:T(4,128)(2,1)}), bf16[8,4,6144]{2,1,0:T(4,128)(2,1)S(1)}, u32[]{:S(2)}, u32[]{:S(2)}) async-start(bf16[8,4,6144]{2,1,0:T(4,128)(2,1)} %reshape.118), calls=%async_computation | async-start | bytes 786432 | tf_op jit(solution)/shard_map/all_to_all | solution.py:88
  40.4 1.9 convolution_convert_fusion.3
  42.4 1.9 reshape.120
  44.3 6.6 %all-to-all-start.1 = ((bf16[8,4,6144]{2,1,0:T(4,128)(2,1)}), bf16[8,4,6144]{2,1,0:T(4,128)(2,1)}, u32[]{:S(2)}, u32[]{:S(2)}) async-start(bf16[8,4,6144]{2,1,0:T(4,128)(2,1)} %reshape.120), calls=%async_computation.1 | async-start | bytes 786432 | tf_op jit(solution)/shard_map/all_to_all | solution.py:88
  55.7 1.9 convolution_convert_fusion.2
  57.7 1.9 reshape.122
  59.5 2.2 all-to-all-done.1
  61.8 4.4 all-to-all-start.2
  68.4 1.9 convolution_convert_fusion.1
  70.4 1.9 reshape.124
  72.9 171.1 %all_gather.7 = bf16[1,2,6144,2]{3,2,1,0:T(8,128)(2,1)} all-gather(bf16[1,2,256,2]{3,2,1,0:T(8,128)(2,1)S(1)} %bitcast.70), channel_id=1, replica_groups=mesh['group'=24,'expert'=8,'tensor'=4] {'group'}, dimensions={2}, use_global_device_ids=true | all-gather | bytes 51200 | tf_op jit(solution)/shard_map/all_gather | solution.py:75
  244.0 8.5 %all-to-all-start.3 = ((bf16[8,4,6144]{2,1,0:T(4,128)(2,1)}), bf16[8,4,6144]{2,1,0:T(4,128)(2,1)}, u32[]{:S(2)}, u32[]{:S(2)}) async-start(bf16[8,4,6144]{2,1,0:T(4,128)(2,1)} %reshape.124), calls=%async_computation.3 | async-start | bytes 786432 | tf_op jit(solution)/shard_map/all_to_all | solution.py:88
  252.6 2.3 bitcast_convert_fusion
  254.9 32.2 %mul.85 = f32[2,6144,2,128]{3,2,1,0:T(2,128)} broadcast(f32[2,6144,2]{2,1,0:T(8,128)S(1)} %bitcast_convert_fusion), dimensions={0,1,2} | broadcast | bytes 12681216 | tf_op jit(solution)/shard_map/mul | solution.py:38
  287.1 16.5 %mul.86 = f32[1,2,6144,256]{3,2,1,0:T(8,128)} reshape(f32[2,6144,2,128]{3,2,1,0:T(2,128)} %mul.85) | data formatting | bytes 25165824 | tf_op jit(solution)/shard_map/mul | solution.py:38
  315.4 9.1 %add_convert_fusion = bf16[1,2,6144,256]{3,2,1,0:T(8,128)(2,1)S(1)} fusion(f32[1,2,6144,256]{3,2,1,0:T(8,128)} %mul.86, bf16[1,2,6144,256]{3,2,1,0:T(8,128)(2,1)} %all-gather.2.cloned.1.call-done, bf16[1,2,6144,256]{3,2,1,0:T(8,128)(2,1)} %param.9), kind=kLoop, calls=%fused_computation | loop fusion | flops 15728640 | bytes 31457280 | tf_op jit(solution)/shard_map/convert_element_type | solution.py:39
  324.5 2.7 copy-done.1
  327.2 2.0 fusion.2
  329.2 5.4 %fusion = bf16[6144,128]{0,1:T(8,128)(2,1)} fusion(bf16[1,256,6144]{2,1,0:T(8,128)(2,1)S(1)} %copy-done, bf16[128,6144]{1,0:T(8,128)(2,1)} %constant_dynamic-update-slice_fusion, bf16[1,2,6144,256]{3,2,1,0:T(8,128)(2,1)} %copy-done.1, f32[128,256]{1,0:T(8,128)S(1)} %fusion.2), kind=kOutput, calls=%fused_computation.2 | convolution fusion | flops 806289408 | bytes 9568256 | tf_op jit(solution)/shard_map/dot_general | solution.py:96
  334.6 59.8 %reduce-scatter.2.cloned.1.call-done = bf16[1536,128]{0,1:T(8,128)(2,1)} async-done(((bf16[6144,128]{0,1:T(8,128)(2,1)}), bf16[1536,128]{0,1:T(8,128)(2,1)}) %reduce-scatter.2.cloned.1.call-update) | async-done | bytes 393232 | tf_op jit(solution)/shard_map/reduce_scatter | solution.py:95
  396.2 6.5 %all-to-all-start.7 = ((bf16[8,4,1536]{2,1,0:T(4,128)(2,1)}), bf16[8,4,1536]{2,1,0:T(4,128)(2,1)S(1)}, u32[]{:S(2)}, u32[]{:S(2)}) async-start(bf16[8,4,1536]{2,1,0:T(4,128)(2,1)} %reshape.132), calls=%async_computation.8 | async-start | bytes 196608 | tf_op jit(solution)/shard_map/all_to_all | solution.py:109
  403.3 7.0 %all-to-all-done.7 = bf16[8,4,1536]{2,1,0:T(4,128)(2,1)S(1)} async-done(((bf16[8,4,1536]{2,1,0:T(4,128)(2,1)}), bf16[8,4,1536]{2,1,0:T(4,128)(2,1)S(1)}, u32[]{:S(2)}, u32[]{:S(2)}) %all-to-all-start.7) | async-done | bytes 98336 | tf_op jit(solution)/shard_map/all_to_all | solution.py:109
  410.2 3.4 all-to-all-start.6
  415.0 6.2 %all-to-all-done.6 = bf16[8,4,1536]{2,1,0:T(4,128)(2,1)S(1)} async-done(((bf16[8,4,1536]{2,1,0:T(4,128)(2,1)}), bf16[8,4,1536]{2,1,0:T(4,128)(2,1)S(1)}, u32[]{:S(2)}, u32[]{:S(2)}) %all-to-all-start.6) | async-done | bytes 98336 | tf_op jit(solution)/shard_map/all_to_all | solution.py:109
  421.2 3.4 all-to-all-start.5
  426.2 5.9 %all-to-all-done.5 = bf16[8,4,1536]{2,1,0:T(4,128)(2,1)S(1)} async-done(((bf16[8,4,1536]{2,1,0:T(4,128)(2,1)}), bf16[8,4,1536]{2,1,0:T(4,128)(2,1)S(1)}, u32[]{:S(2)}, u32[]{:S(2)}) %all-to-all-start.5) | async-done | bytes 98336 | tf_op jit(solution)/shard_map/all_to_all | solution.py:109
  432.2 3.4 all-to-all-start.4
  435.9 7.1 %all-to-all-done.4 = bf16[8,4,1536]{2,1,0:T(4,128)(2,1)S(1)} async-done(((bf16[8,4,1536]{2,1,0:T(4,128)(2,1)}), bf16[8,4,1536]{2,1,0:T(4,128)(2,1)S(1)}, u32[]{:S(2)}, u32[]{:S(2)}) %all-to-all-start.4) | async-done | bytes 98336 | tf_op jit(solution)/shard_map/all_to_all | solution.py:109
  (95 shorter events, 43.7 us)
Async XLA Ops:
  6.5 322.7 %copy-start = (bf16[1,256,6144]{2,1,0:T(8,128)(2,1)S(1)}, bf16[1,256,6144]{2,1,0:T(8,128)(2,1)}, u32[]{:S(2)}) copy-start(bf16[1,256,6144]{2,1,0:T(8,128)(2,1)} %param.11) | copy-start | bytes 9437188
  6.5 308.8 %all-gather.2.cloned.1.call-start = ((), (), s32[]{:S(2)}) async-start(), calls=%async_computation.9 | async-start | bytes 6553600 | tf_op jit(solution)/shard_map/all_gather | solution.py:75
  6.5 11.5 %copy-start.8 = (s32[4,8,2]{1,2,0:T(2,128)S(1)}, s32[4,8,2]{1,2,0:T(2,128)}, u32[]{:S(2)}) copy-start(s32[4,8,2]{1,2,0:T(2,128)} %param.7) | copy-start | bytes 772
  12.1 0.6 copy-start.3
  19.2 0.5 copy-start.4
  21.9 22.3 %all-to-all-start = ((bf16[8,4,6144]{2,1,0:T(4,128)(2,1)}), bf16[8,4,6144]{2,1,0:T(4,128)(2,1)S(1)}, u32[]{:S(2)}, u32[]{:S(2)}) async-start(bf16[8,4,6144]{2,1,0:T(4,128)(2,1)} %reshape.118), calls=%async_computation | async-start | bytes 786432 | tf_op jit(solution)/shard_map/all_to_all | solution.py:88
  29.8 1.4 copy-start.7
  38.5 27.7 %copy-start.2 = (s32[16,8]{1,0:T(8,128)S(1)}, s32[16,8]{1,0:T(8,128)}, u32[]{:S(2)}) copy-start(s32[16,8]{1,0:T(8,128)} %reduce_window_sum.32) | copy-start | bytes 1540
  44.3 17.5 %all-to-all-start.1 = ((bf16[8,4,6144]{2,1,0:T(4,128)(2,1)}), bf16[8,4,6144]{2,1,0:T(4,128)(2,1)}, u32[]{:S(2)}, u32[]{:S(2)}) async-start(bf16[8,4,6144]{2,1,0:T(4,128)(2,1)} %reshape.120), calls=%async_computation.1 | async-start | bytes 786432 | tf_op jit(solution)/shard_map/all_to_all | solution.py:88
  55.7 11.9 %copy-start.5 = (s32[1,8,2]{1,2,0:T(2,128)}, s32[1,8,2]{1,2,0:T(2,128)S(1)}, u32[]{:S(2)}) copy-start(s32[1,8,2]{1,2,0:T(2,128)S(1)} %copy.44) | copy-start | bytes 196
  61.8 182.3 %all-to-all-start.2 = ((bf16[8,4,6144]{2,1,0:T(4,128)(2,1)}), bf16[8,4,6144]{2,1,0:T(4,128)(2,1)}, u32[]{:S(2)}, u32[]{:S(2)}) async-start(bf16[8,4,6144]{2,1,0:T(4,128)(2,1)} %reshape.122), calls=%async_computation.2 | async-start | bytes 786432 | tf_op jit(solution)/shard_map/all_to_all | solution.py:88
  244.0 63.3 %all-to-all-start.3 = ((bf16[8,4,6144]{2,1,0:T(4,128)(2,1)}), bf16[8,4,6144]{2,1,0:T(4,128)(2,1)}, u32[]{:S(2)}, u32[]{:S(2)}) async-start(bf16[8,4,6144]{2,1,0:T(4,128)(2,1)} %reshape.124), calls=%async_computation.3 | async-start | bytes 786432 | tf_op jit(solution)/shard_map/all_to_all | solution.py:88
  252.6 141.9 %reduce-scatter.2.cloned.1.call-start = ((), (), s32[]{:S(2)}) async-start(), calls=%async_computation.10 | async-start | bytes 1966080 | tf_op jit(solution)/shard_map/reduce_scatter | solution.py:95
  324.5 2.7 copy-start.1
  334.6 79.0 %copy-start.9 = (f32[4,8,2]{1,2,0:T(2,128)S(1)}, f32[4,8,2]{1,2,0:T(2,128)}, u32[]{:S(2)}) copy-start(f32[4,8,2]{1,2,0:T(2,128)} %param.8) | copy-start | bytes 772
  334.6 79.6 %copy-start.6 = (s32[1,8,2]{1,2,0:T(2,128)S(1)}, s32[1,8,2]{1,2,0:T(2,128)}, u32[]{:S(2)}) copy-start(s32[1,8,2]{1,2,0:T(2,128)} %copy-done.5) | copy-start | bytes 196
  396.2 14.1 %all-to-all-start.7 = ((bf16[8,4,1536]{2,1,0:T(4,128)(2,1)}), bf16[8,4,1536]{2,1,0:T(4,128)(2,1)S(1)}, u32[]{:S(2)}, u32[]{:S(2)}) async-start(bf16[8,4,1536]{2,1,0:T(4,128)(2,1)} %reshape.132), calls=%async_computation.8 | async-start | bytes 196608 | tf_op jit(solution)/shard_map/all_to_all | solution.py:109
  410.2 11.0 %all-to-all-start.6 = ((bf16[8,4,1536]{2,1,0:T(4,128)(2,1)}), bf16[8,4,1536]{2,1,0:T(4,128)(2,1)S(1)}, u32[]{:S(2)}, u32[]{:S(2)}) async-start(bf16[8,4,1536]{2,1,0:T(4,128)(2,1)} %reshape.130), calls=%async_computation.7 | async-start | bytes 196608 | tf_op jit(solution)/shard_map/all_to_all | solution.py:109
  421.2 11.0 %all-to-all-start.5 = ((bf16[8,4,1536]{2,1,0:T(4,128)(2,1)}), bf16[8,4,1536]{2,1,0:T(4,128)(2,1)S(1)}, u32[]{:S(2)}, u32[]{:S(2)}) async-start(bf16[8,4,1536]{2,1,0:T(4,128)(2,1)} %reshape.128), calls=%async_computation.6 | async-start | bytes 196608 | tf_op jit(solution)/shard_map/all_to_all | solution.py:109
  432.2 10.9 %all-to-all-start.4 = ((bf16[8,4,1536]{2,1,0:T(4,128)(2,1)}), bf16[8,4,1536]{2,1,0:T(4,128)(2,1)S(1)}, u32[]{:S(2)}, u32[]{:S(2)}) async-start(bf16[8,4,1536]{2,1,0:T(4,128)(2,1)} %reshape.126), calls=%async_computation.5 | async-start | bytes 196608 | tf_op jit(solution)/shard_map/all_to_all | solution.py:109
Sparse Core Ops, SparseCore 0:
  18.1 230.9 all-gather.1
  334.7 59.6 reduce-scatter.1
where the time goes:
time: 456 us; the launch traced here: 451 us
  blocking collectives  171 us (38%)
  local copies, waits for them, and re-layouts  89.2 us (20%)
  waiting for transfers between devices  88.3 us (19%)
  starting transfers between devices  43.8 us (10%)
  other arithmetic  29.6 us (6%)
  matrix products  15 us (3%)
  between operations  13.6 us (3%)
    all_gather x1, blocking collectives, shards(): lax.all_gather((levels, per_row), 'group', axis=2, tiled=True)  171 us
    reduce_scatter x1, waiting for transfers between devices, shards(): lax.psum_scatter(lax.dot_general(columns, hidden, (((0,), (1,)), ((), ())...  59.8 us
    mul x2, local copies, waits for them, and re-layouts, apply_levels(): added = (expanded * step_size).reshape(current.shape)  48.7 us
    all_to_all x4, starting transfers between devices, shards(): lax.all_to_all(outgoing, 'expert', split_axis=0, concat_axis=0, tiled=True)  27.3 us
    all_to_all x4, waiting for transfers between devices, shards(): lax.all_to_all(expert_out, 'expert', split_axis=0, concat_axis=0, tiled=T...  26.3 us
    all_to_all x4, starting transfers between devices, shards(): lax.all_to_all(expert_out, 'expert', split_axis=0, concat_axis=0, tiled=T...  16.5 us
    unnamed x27, local copies, waits for them, and re-layouts  9.75 us
    convert_element_type x1, other arithmetic, apply_levels(): return (current.astype(jnp.float32) + added).astype(jnp.bfloat16)  9.12 us
  transfers between devices with their start and end apart: 10, of which 6 were waited for; matrix products, arithmetic and copies ran while one was open for 22% of the time, Pallas kernels for 0%

commit v1 on v0

v1 whole, which is shorter than its diff:
```python
import jax
import jax.numpy as jnp
from jax import lax
from jax.experimental import pallas as pl
from jax.experimental.pallas import tpu as pltpu
from jax.sharding import Mesh
from jax.sharding import PartitionSpec as P

BLOCK = 128
CAP = 4
STEP_SLOTS = 16
ORDER = (0, -1, 1, 2)
PARTS = 6
VMEM_BYTES = 48 * 1024 * 1024

clip_level = 2.0
epsilon = 1e-06


def sync_kernel(place, learner, rollout, out):
    core = place[0]
    units = learner.shape[3]
    for half in range(learner.shape[2] // BLOCK):
        rows = pl.ds(pl.multiple_of((half ^ core) * BLOCK, BLOCK), BLOCK)
        for matrix in range(2):
            for column in range(units // BLOCK):
                columns = pl.ds(column * BLOCK, BLOCK)
                current = rollout[0, matrix, rows, columns].astype(jnp.float32)
                change = learner[0, matrix, rows, columns] - current
                mean_square = jnp.sum(change * change, keepdims=True) * (1.0 / (BLOCK * BLOCK))
                scale = jnp.sqrt(mean_square + epsilon).astype(jnp.bfloat16).astype(jnp.float32)
                levels = jnp.clip(change / scale, -clip_level, clip_level)
                levels = levels.astype(jnp.bfloat16).astype(jnp.float32)
                out[half, :, pl.ds(matrix * units + column * BLOCK, BLOCK)] = (
                    current + levels * scale
                ).astype(jnp.bfloat16)


def slot_choice(first, second, experts, steps):
    rows = first.shape[0]
    per_step = rows // steps
    slots = experts * steps * CAP
    row = lax.broadcasted_iota(jnp.int32, (rows, slots), 0)
    slot = lax.broadcasted_iota(jnp.int32, (rows, slots), 1)
    expert = (slot // (steps * CAP)).astype(jnp.float32)
    from_first, from_second = first == expert, second == expert
    named = (from_first | from_second).astype(jnp.float32)
    later = lax.broadcasted_iota(jnp.int32, (rows, rows), 0)
    earlier = lax.broadcasted_iota(jnp.int32, (rows, rows), 1)
    before = (earlier < later) & (earlier // per_step == later // per_step)
    rank = jnp.dot(
        before.astype(jnp.bfloat16), named.astype(jnp.bfloat16), preferred_element_type=jnp.float32
    )
    here = (slot // CAP % steps == row // per_step) & (rank == (slot % CAP).astype(jnp.float32))
    return from_first & here, from_second & here


def pack_kernel(place, ids, gates, tokens, outgoing, combine):
    core, z_high = place[0], place[3]
    sign = 1 - 2 * core
    parts, rows, columns = outgoing.shape
    pieces = columns // BLOCK - 1
    steps = rows // 8
    experts = combine.shape[1] // (steps * CAP)
    first, second = ids[:, 0:1].astype(jnp.float32), ids[:, 1:2].astype(jnp.float32)
    chosen_first, chosen_second = slot_choice(first, second, experts, steps)
    combine[...] = jnp.where(chosen_first, gates[:, 0:1], 0.0) + jnp.where(
        chosen_second, gates[:, 1:2], 0.0
    )
    lane = lax.broadcasted_iota(jnp.int32, (rows, BLOCK), 1)
    tail = jnp.where(lane == 0, first, jnp.where(lane == 1, second, 0.0)).astype(jnp.bfloat16)
    for part in range(parts):
        for piece in range(pieces):
            owner = lax.rem(z_high + sign * ORDER[piece] + pieces, pieces)
            start = ((owner * parts + part) * 2 + core) * BLOCK
            outgoing[part, :, piece * BLOCK : (piece + 1) * BLOCK] = tokens[
                :, pl.ds(pl.multiple_of(start, BLOCK), BLOCK)
            ]
        outgoing[part, :, pieces * BLOCK :] = tail


def dispatch_kernel(arrived, outgoing):
    experts, parts, step_slots, columns = outgoing.shape
    steps = step_slots // CAP
    for part in range(parts):
        tail = arrived[part, :, columns:].astype(jnp.float32)
        chosen_first, chosen_second = slot_choice(tail[:, 0:1], tail[:, 1:2], experts, steps)
        select = (chosen_first | chosen_second).astype(jnp.float32).astype(jnp.bfloat16)
        moved = lax.dot_general(
            select,
            arrived[part, :, :columns],
            (((0,), (0,)), ((), ())),
            preferred_element_type=jnp.float32,
        ).astype(jnp.bfloat16)
        for expert in range(experts):
            outgoing[expert, part] = moved[expert * step_slots : (expert + 1) * step_slots]


def gate_up_kernel(own, other, here, first, second, far, out):
    total = None
    for piece, (across, weights) in enumerate(((0, here), (2, first), (1, second), (3, far))):
        rows = jnp.concatenate(
            [
                own[:, piece * BLOCK : (piece + 1) * BLOCK],
                other[:, across * BLOCK : (across + 1) * BLOCK],
            ],
            axis=1,
        )
        term = jnp.dot(
            rows,
            weights[...].reshape(2 * BLOCK, weights.shape[2]),
            preferred_element_type=jnp.float32,
        )
        total = term if total is None else total + term
    partial = total.astype(jnp.bfloat16)
    parts, slots, _ = out.shape
    experts = own.shape[0] // (parts * STEP_SLOTS)
    for expert in range(experts):
        for part in range(parts):
            at = (expert * parts + part) * STEP_SLOTS
            out[part, expert * STEP_SLOTS : (expert + 1) * STEP_SLOTS] = partial[
                at : at + STEP_SLOTS
            ]


def down_kernel(place, hidden, own, crossed, sibling, out):
    units = own.shape[1]
    tensor = place[1]
    total = None
    for flip, columns in enumerate((own[0], sibling[0], crossed[...], sibling[1])):
        at = pl.ds(pl.multiple_of((tensor ^ flip) * units, units), units)
        term = jnp.dot(hidden[:, at], columns, preferred_element_type=jnp.float32)
        total = term if total is None else total + term
    out[...] = total.astype(jnp.bfloat16)


def shards(tokens, expert_ids, gate_values, rollout_gate_up, learner_gate_up, down_weight):
    ring = lax.axis_size("z_hi")
    expert_count = lax.axis_size("expert")
    tensor_count = lax.axis_size(("x_hi", "core"))
    step_count, token_count, width = tokens.shape
    quarter = width // tensor_count
    own_rows, units = learner_gate_up.shape[2:]
    slots = expert_count * step_count * CAP
    tensor = lax.axis_index(("x_hi", "core"))
    group = lax.axis_index(("z_hi", "z_lo", "x_lo"))
    place = jnp.stack([tensor % 2, tensor, group, group // PARTS]).astype(jnp.int32)

    def whole(*shape):
        return pl.BlockSpec(shape, lambda i, p: (0,) * len(shape))

    def call(body, out_shape, in_specs, out_specs, name):
        return pl.pallas_call(
            body,
            grid_spec=pltpu.PrefetchScalarGridSpec(
                num_scalar_prefetch=1, grid=(1,), in_specs=in_specs, out_specs=out_specs
            ),
            out_shape=out_shape,
            compiler_params=pltpu.CompilerParams(vmem_limit_bytes=VMEM_BYTES),
            name=name,
        )

    flat_tokens = tokens.reshape(step_count * token_count, width)
    rows = step_count * token_count
    packed, combine = call(
        pack_kernel,
        [
            jax.ShapeDtypeStruct((PARTS, rows, (ring + 1) * BLOCK), jnp.bfloat16),
            jax.ShapeDtypeStruct((rows, slots), jnp.float32),
        ],
        [whole(rows, 2), whole(rows, 2), whole(rows, width)],
        [whole(PARTS, rows, (ring + 1) * BLOCK), whole(rows, slots)],
        "pack_rows",
    )(place, expert_ids.reshape(rows, 2), gate_values.reshape(rows, 2), flat_tokens)
    shared = lax.all_to_all(packed, ("z_lo", "x_lo"), split_axis=0, concat_axis=0, tiled=True)

    packed, learner_gate_up = lax.optimization_barrier((packed, learner_gate_up))
    synced = call(
        sync_kernel,
        jax.ShapeDtypeStruct((2, own_rows // 2, 2 * units), jnp.bfloat16),
        [
            whole(1, 2, own_rows, units),
            pl.BlockSpec((1, 2, own_rows, units), lambda i, p: (0, 0, p[2], 0)),
        ],
        whole(2, own_rows // 2, 2 * units),
        "sync_rows",
    )(place, learner_gate_up, rollout_gate_up)

    def along(value, sign):
        perm = [
            (i * 2 + core, (i + sign * (1 - 2 * core)) % ring * 2 + core)
            for i in range(ring)
            for core in range(2)
        ]
        return lax.ppermute(value, ("z_hi", "core"), perm)

    first = along(synced, 1)
    second = along(synced, -1)

    synced, shared = lax.optimization_barrier((synced, shared))
    outgoing = pl.pallas_call(
        dispatch_kernel,
        out_shape=jax.ShapeDtypeStruct(
            (expert_count, PARTS, step_count * CAP, ring * BLOCK), jnp.bfloat16
        ),
        compiler_params=pltpu.CompilerParams(vmem_limit_bytes=VMEM_BYTES),
        name="dispatch_rows",
    )(shared)
    outgoing, first = lax.optimization_barrier((outgoing, first))
    far = along(first, 1)
    arrived = lax.all_to_all(outgoing, "expert", split_axis=0, concat_axis=0, tiled=True)
    arrived, second, far = lax.optimization_barrier((arrived, second, far))
    own = arrived.reshape(PARTS * slots, ring * BLOCK)
    other = lax.ppermute(own, "core", [(0, 1), (1, 0)])

    crossed = lax.ppermute(
        lax.dynamic_slice_in_dim(down_weight[0], (1 - tensor // 2) * 2 * quarter, 2 * quarter, 1),
        ("x_lo", "x_hi", "core"),
        [(i, i ^ 6) for i in range(8)],
    )
    sibling = lax.ppermute(
        jnp.stack(
            [
                lax.dynamic_slice_in_dim(down_weight[0], (tensor ^ 1) * quarter, quarter, 1),
                lax.dynamic_slice_in_dim(crossed, (1 - tensor % 2) * quarter, quarter, 1),
            ]
        ),
        "core",
        [(0, 1), (1, 0)],
    )

    partial = pl.pallas_call(
        gate_up_kernel,
        out_shape=jax.ShapeDtypeStruct((PARTS, slots, 2 * units), jnp.bfloat16),
        compiler_params=pltpu.CompilerParams(vmem_limit_bytes=VMEM_BYTES),
        name="gate_up",
    )(own, other, synced, first, second, far)
    partial = lax.all_to_all(partial, ("z_lo", "x_lo"), split_axis=0, concat_axis=0, tiled=True)
    both = jnp.sum(partial.astype(jnp.float32), axis=0)
    hidden = (jax.nn.silu(both[:, :units]) * both[:, units:]).astype(jnp.bfloat16)
    hidden = lax.all_gather(hidden, ("x_hi", "core"), axis=1, tiled=True)
    expert_out = call(
        down_kernel,
        jax.ShapeDtypeStruct((slots, quarter), jnp.bfloat16),
        [
            whole(slots, tensor_count * units),
            pl.BlockSpec((1, units, quarter), lambda i, p: (0, 0, p[1])),
            pl.BlockSpec((units, quarter), lambda i, p: (0, p[0])),
            whole(2, units, quarter),
        ],
        whole(slots, quarter),
        "down",
    )(place, hidden, down_weight, crossed, sibling)
    back = lax.all_to_all(
        expert_out.reshape(expert_count, step_count * CAP, quarter),
        "expert",
        split_axis=0,
        concat_axis=0,
        tiled=True,
    )
    mixed = jnp.dot(
        combine,
        back.reshape(slots, quarter).astype(jnp.float32),
        precision=lax.Precision.HIGHEST,
    )
    return mixed.astype(jnp.bfloat16).reshape(step_count, token_count, quarter)


def solution(mesh):
    groups, experts, tensors = mesh.devices.shape
    split = Mesh(
        mesh.devices.reshape(groups // PARTS, PARTS // 2, 2, experts, tensors // 2, 2),
        ("z_hi", "z_lo", "x_lo", "expert", "x_hi", "core"),
    )
    group, tensor = ("z_hi", "z_lo", "x_lo"), ("x_hi", "core")
    in_specs = (
        P(None, (*group, "expert"), None),
        P(None, (*group, "expert"), None),
        P(None, (*group, "expert"), None),
        P("expert", None, None, tensor),
        P("expert", None, group, tensor),
        P("expert", tensor, None),
    )
    out_specs = P(None, (*group, "expert"), tensor)
    return jax.shard_map(shards, mesh=split, in_specs=in_specs, out_specs=out_specs, check_vma=False)
```

time: 456 us -> 135 us (0.30)
  blocking collectives: 171 us -> 30.1 us
  local copies, waits for them, and re-layouts: 89.2 us -> 7.52 us
  waiting for transfers between devices: 88.3 us -> 34.2 us
  other arithmetic: 29.6 us -> 2.69 us
  matrix products: 15 us -> 0.92 us
  between operations: 13.6 us -> 0.14 us
  Pallas kernels: 0 us -> 9.75 us
  starting transfers between devices: 43.8 us -> 48.7 us
    all_gather x1, blocking collectives: 171 us -> 8.33 us  [shards(): hidden = lax.all_gather(hidden, ('x_hi', 'core'), axis=1, tiled=True)]
    reduce_scatter x1 -> x0, waiting for transfers between devices: 59.8 us -> none  [shards(): lax.psum_scatter(lax.dot_general(columns, hidden, (((0,), (1,)), ((), ())...]
    mul x3 -> x0, local copies, waits for them, and re-layouts: 50.8 us -> none  [the longest x2 48.7 us: apply_levels(): added = (expanded * step_size).reshape(current.shape)]
    ppermute x0 -> x6, starting transfers between devices: none -> 30.8 us  [the longest x3 21.5 us: along(): return lax.ppermute(value, ('z_hi', 'core'), perm)]
    ppermute x0 -> x6, waiting for transfers between devices: none -> 24.7 us  [the longest x3 22.8 us: along(): return lax.ppermute(value, ('z_hi', 'core'), perm)]
    all_to_all x0 -> x1, blocking collectives: none -> 21.8 us  [shards(): lax.all_to_all(expert_out.reshape(expert_count, step_count * CAP, quarter...]
    all_to_all x4 -> x1, starting transfers between devices: 27.3 us -> 6.82 us  [shards(): lax.all_to_all(outgoing, 'expert', split_axis=0, concat_axis=0, tiled=True)]
    all_to_all x4 -> x2, waiting for transfers between devices: 26.3 us -> 9.46 us  [the longest x1 9.46 us: shards(): lax.all_to_all(partial, ('z_lo', 'x_lo'), split_axis=0, concat_axis=0, ti...]
  transfers between devices with their start and end apart: 10 -> 9, of which waited for: 6 -> 5; matrix products, arithmetic and copies ran while one was open for 22% -> 5% of each run, Pallas kernels for 0% -> 5%
where the time goes in v1:
time: 135 us; the launch traced here: 134 us
  starting transfers between devices  48.7 us (36%)
  waiting for transfers between devices  34.2 us (25%)
  blocking collectives  30.1 us (22%)
  Pallas kernels  9.75 us (7%)
  local copies, waits for them, and re-layouts  7.52 us (6%)
  other arithmetic  2.69 us (2%)
    ppermute x3, waiting for transfers between devices, along(): return lax.ppermute(value, ('z_hi', 'core'), perm)  22.8 us
    all_to_all x1, blocking collectives, shards(): lax.all_to_all(expert_out.reshape(expert_count, step_count * CAP, quarter...  21.8 us
    ppermute x3, starting transfers between devices, along(): return lax.ppermute(value, ('z_hi', 'core'), perm)  21.5 us
    all_to_all x1, waiting for transfers between devices, shards(): lax.all_to_all(partial, ('z_lo', 'x_lo'), split_axis=0, concat_axis=0, ti...  9.46 us
    all_gather x1, blocking collectives, shards(): hidden = lax.all_gather(hidden, ('x_hi', 'core'), axis=1, tiled=True)  8.33 us
    all_to_all x1, starting transfers between devices, shards(): lax.all_to_all(packed, ('z_lo', 'x_lo'), split_axis=0, concat_axis=0, til...  6.93 us
    all_to_all x1, starting transfers between devices, shards(): lax.all_to_all(outgoing, 'expert', split_axis=0, concat_axis=0, tiled=True)  6.82 us
    ppermute x1, starting transfers between devices, shards(): lax.ppermute(lax.dynamic_slice_in_dim(down_weight[0], (1 - tensor // 2) *...  4.58 us
  transfers between devices with their start and end apart: 9, of which 5 were waited for; matrix products, arithmetic and copies ran while one was open for 5% of the time, Pallas kernels for 5%

profile of v1, /device:TPU:1, one launch (start us, length us, event | category | flops | bytes accessed | tf_op | source)
XLA Modules:
  0.0 134.1 jit_solution(5820081960484118202)
XLA Ops:
  0.0 0.8 copy.11
  0.8 0.8 copy.12
  1.6 0.1 pad_add_fusion.place
  1.6 1.0 copy-done.1
  2.6 1.3 %pack_rows.1 = (bf16[6,32,640]{2,1,0:T(8,128)(2,1)}, f32[32,128]{1,0:T(8,128)S(1)}) custom-call(s32[4]{0:T(128)S(1)} %pad_add_fusion.place, s32[32,2]{1,0:T(8,128)S(1)} %bitcast.22, f32[32,2]{1,0:T(8,128)S(1)} %bitcast.23, bf16[32,6144]{1,0:T(8,128)(2,1)S(1)} %bitcast.21), custom_call_target="tpu_custom_call" | custom-call | tf_op jit(solution)/shard_map/pack_rows/pallas_call | solution.py:165
  4.0 6.9 %all-to-all-start = ((bf16[6,32,640]{2,1,0:T(8,128)(2,1)}), bf16[6,32,640]{2,1,0:T(8,128)(2,1)S(1)}, u32[]{:S(2)}, u32[]{:S(2)}) async-start(bf16[6,32,640]{2,1,0:T(8,128)(2,1)} %get-tuple-element.16), calls=%async_computation | async-start | bytes 491520 | tf_op jit(solution)/shard_map/all_to_all | solution.py:175
  10.9 1.0 copy-done
  12.0 1.8 %sync_rows.1.here = bf16[2,128,512]{2,1,0:T(8,128)(2,1)S(1)} custom-call(s32[4]{0:T(128)S(1)} %pad_add_fusion.place, f32[1,2,256,256]{3,2,1,0:T(8,128)S(1)} %copy-done, bf16[1,2,6144,256]{3,2,1,0:T(8,128)(2,1)} %rollout.1), custom_call_target="tpu_custom_call" | custom-call | tf_op jit(solution)/shard_map/sync_rows/pallas_call | solution.py:178
  13.8 12.5 %collective-permute-start = (bf16[2,128,512]{2,1,0:T(8,128)(2,1)S(1)}, bf16[2,128,512]{2,1,0:T(8,128)(2,1)S(1)}, u32[]{:S(2)}, u32[]{:S(2)}) collective-permute-start(bf16[2,128,512]{2,1,0:T(8,128)(2,1)S(1)} %sync_rows.1.here), channel_id=1, source_target_pairs={{0,192},{1,577},{192,384},{193,1},{384,576},{385,193},{576,0},{577... | collective-permute-start | bytes 786440 | tf_op jit(solution)/shard_map/ppermute | solution.py:195
  26.3 2.4 %dispatch_rows.1 = bf16[8,6,16,512]{3,2,1,0:T(8,128)(2,1)} custom-call(bf16[6,32,640]{2,1,0:T(8,128)(2,1)S(1)} %all-to-all-done.arrived), custom_call_target="tpu_custom_call" | custom-call | tf_op jit(solution)/shard_map/dispatch_rows/pallas_call | solution.py:201
  28.7 6.5 %collective-permute-done.first = bf16[2,128,512]{2,1,0:T(8,128)(2,1)S(1)} collective-permute-done((bf16[2,128,512]{2,1,0:T(8,128)(2,1)S(1)}, bf16[2,128,512]{2,1,0:T(8,128)(2,1)S(1)}, u32[]{:S(2)}, u32[]{:S(2)}) %collective-permute-start) | collective-permute-done | bytes 262176 | tf_op jit(solution)/shard_map/ppermute | solution.py:195
  35.2 6.8 %all-to-all-start.1 = ((bf16[8,6,16,512]{3,2,1,0:T(8,128)(2,1)}), bf16[8,6,16,512]{3,2,1,0:T(8,128)(2,1)S(1)}, u32[]{:S(2)}, u32[]{:S(2)}) async-start(bf16[8,6,16,512]{3,2,1,0:T(8,128)(2,1)} %dispatch_rows.1), calls=%async_computation.1 | async-start | bytes 1572864 | tf_op jit(solution)/shard_map/all_to_all | solution.py:211
  42.1 2.7 %dynamic-slice_bitcast_fusion = bf16[256,3072]{1,0:T(8,128)(2,1)} fusion(bf16[1,256,6144]{2,1,0:T(8,128)(2,1)} %own.1, s32[]{:T(128)S(6)} %select_n.28), kind=kLoop, calls=%fused_computation.3 | loop fusion | bytes 3145732 | tf_op jit(solution)/shard_map/dynamic_slice | solution.py:217
  44.7 4.6 %collective-permute-start.4 = (bf16[256,3072]{1,0:T(8,128)(2,1)}, bf16[256,3072]{1,0:T(8,128)(2,1)S(1)}, u32[]{:S(2)}, u32[]{:S(2)}) collective-permute-start(bf16[256,3072]{1,0:T(8,128)(2,1)} %dynamic-slice_bitcast_fusion), channel_id=1, source_target_pairs={{0,34},{1,35},{2,32},{3,33},{32,2},{33,3},{34,0},{35,1},{4,38},{5,... | collective-permute-start | bytes 4718600 | tf_op jit(solution)/shard_map/ppermute | solution.py:216
  49.3 2.5 %collective-permute-start.1 = (bf16[2,128,512]{2,1,0:T(8,128)(2,1)S(1)}, bf16[2,128,512]{2,1,0:T(8,128)(2,1)S(1)}, u32[]{:S(2)}, u32[]{:S(2)}) collective-permute-start(bf16[2,128,512]{2,1,0:T(8,128)(2,1)S(1)} %sync_rows.1.here), channel_id=1, source_target_pairs={{0,576},{1,193},{192,0},{193,385},{384,192},{385,577},{576,384},{5... | collective-permute-start | bytes 786440 | tf_op jit(solution)/shard_map/ppermute | solution.py:195
  51.9 6.5 %collective-permute-start.2 = (bf16[2,128,512]{2,1,0:T(8,128)(2,1)S(1)}, bf16[2,128,512]{2,1,0:T(8,128)(2,1)S(1)}, u32[]{:S(2)}, u32[]{:S(2)}) collective-permute-start(bf16[2,128,512]{2,1,0:T(8,128)(2,1)S(1)} %collective-permute-done.first), channel_id=1, source_target_pairs={{0,192},{1,577},{192,384},{193,1},{384,576},{385,193},{576,0},{577... | collective-permute-start | bytes 786440 | tf_op jit(solution)/shard_map/ppermute | solution.py:195
  58.4 5.5 %collective-permute-done.1.second = bf16[2,128,512]{2,1,0:T(8,128)(2,1)S(1)} collective-permute-done((bf16[2,128,512]{2,1,0:T(8,128)(2,1)S(1)}, bf16[2,128,512]{2,1,0:T(8,128)(2,1)S(1)}, u32[]{:S(2)}, u32[]{:S(2)}) %collective-permute-start.1) | collective-permute-done | bytes 262176 | tf_op jit(solution)/shard_map/ppermute | solution.py:195
  63.9 10.8 %collective-permute-done.2.far = bf16[2,128,512]{2,1,0:T(8,128)(2,1)S(1)} collective-permute-done((bf16[2,128,512]{2,1,0:T(8,128)(2,1)S(1)}, bf16[2,128,512]{2,1,0:T(8,128)(2,1)S(1)}, u32[]{:S(2)}, u32[]{:S(2)}) %collective-permute-start.2) | collective-permute-done | bytes 262176 | tf_op jit(solution)/shard_map/ppermute | solution.py:195
  74.7 2.4 %collective-permute-start.3 = (bf16[768,512]{1,0:T(8,128)(2,1)S(1)}, bf16[768,512]{1,0:T(8,128)(2,1)S(1)}, u32[]{:S(2)}, u32[]{:S(2)}) collective-permute-start(bf16[768,512]{1,0:T(8,128)(2,1)S(1)} %bitcast.18), channel_id=1, source_target_pairs={{0,1},{1,0},{2,3},{3,2},{4,5},{5,4},{6,7},{7,6},{8,9},{9,8},{10,11... | collective-permute-start | bytes 2359304 | tf_op jit(solution)/shard_map/ppermute | solution.py:214
  77.1 1.9 %collective-permute-done.3.other = bf16[768,512]{1,0:T(8,128)(2,1)S(1)} collective-permute-done((bf16[768,512]{1,0:T(8,128)(2,1)S(1)}, bf16[768,512]{1,0:T(8,128)(2,1)S(1)}, u32[]{:S(2)}, u32[]{:S(2)}) %collective-permute-start.3) | collective-permute-done | bytes 786464 | tf_op jit(solution)/shard_map/ppermute | solution.py:214
  79.0 1.9 %gate_up.1 = bf16[6,128,512]{2,1,0:T(8,128)(2,1)} custom-call(bf16[768,512]{1,0:T(8,128)(2,1)S(1)} %bitcast.19, bf16[768,512]{1,0:T(8,128)(2,1)S(1)} %collective-permute-done.3.other, bf16[2,128,512]{2,1,0:T(8,128)(2,1)S(1)} %sync_rows.1.here, bf16[2,128,512]{2,1,0:T(8,128)(2,1)S(1)} %collective-permute-done.first, ...), custom_call_target="tpu_custom_call" | custom-call | tf_op jit(solution)/shard_map/gate_up/pallas_call | solution.py:232
  80.9 4.2 %all-to-all-start.2 = ((bf16[6,128,512]{2,1,0:T(8,128)(2,1)}), bf16[6,128,512]{2,1,0:T(8,128)(2,1)}, u32[]{:S(2)}, u32[]{:S(2)}) async-start(bf16[6,128,512]{2,1,0:T(8,128)(2,1)} %gate_up.1), calls=%async_computation.2 | async-start | bytes 1572864 | tf_op jit(solution)/shard_map/all_to_all | solution.py:238
  85.1 1.2 constant_dynamic-slice_fusion
  86.3 0.1 dynamic-slice_bitcast_fusion.1
  86.4 1.3 pad_maximum_fusion
  87.7 2.3 %collective-permute-start.5 = (bf16[2,256,1536]{2,1,0:T(8,128)(2,1)}, bf16[2,256,1536]{2,1,0:T(8,128)(2,1)S(1)}, u32[]{:S(2)}, u32[]{:S(2)}) collective-permute-start(bf16[2,256,1536]{2,1,0:T(8,128)(2,1)} %pad_maximum_fusion), channel_id=1, source_target_pairs={{0,1},{1,0},{2,3},{3,2},{4,5},{5,4},{6,7},{7,6},{8,9},{9,8},{10,11... | collective-permute-start | bytes 4718600 | tf_op jit(solution)/shard_map/ppermute | solution.py:221
  90.0 9.5 %all-to-all-done.2 = bf16[6,128,512]{2,1,0:T(8,128)(2,1)} async-done(((bf16[6,128,512]{2,1,0:T(8,128)(2,1)}), bf16[6,128,512]{2,1,0:T(8,128)(2,1)}, u32[]{:S(2)}, u32[]{:S(2)}) %all-to-all-start.2) | async-done | bytes 786464 | tf_op jit(solution)/shard_map/all_to_all | solution.py:238
  99.4 1.3 convert_reduce_fusion
  100.7 8.3 %all_gather.3.hidden = bf16[128,1024]{1,0:T(8,128)(2,1)S(1)} all-gather(bf16[128,256]{1,0:T(8,128)(2,1)S(1)} %fusion.1), channel_id=1, replica_groups=mesh['z_hi'=4,'z_lo'=3,'x_lo'=2,'expert'=8,'x_hi'=2,'core'=2] {'x_hi','c..., dimensions={1}, use_global_device_ids=true | all-gather | bytes 327680 | tf_op jit(solution)/shard_map/all_gather | solution.py:241
  109.1 2.3 %down.1 = bf16[128,1536]{1,0:T(8,128)(2,1)S(1)} custom-call(s32[4]{0:T(128)S(1)} %pad_add_fusion.place, bf16[128,1024]{1,0:T(8,128)(2,1)S(1)} %all_gather.3.hidden, bf16[1,256,6144]{2,1,0:T(8,128)(2,1)} %own.1, bf16[256,3072]{1,0:T(8,128)(2,1)S(1)} %collective-permute-done.4.crossed, bf16[2,256,1536]{2,1,0:T(8,128)(2,1)S(1)} %collective-permute-done.5.sibling), custom_call_target="tpu_custom_call" | custom-call | tf_op jit(solution)/shard_map/down/pallas_call | solution.py:242
  111.3 21.8 %all_to_all.20 = bf16[8,16,1536]{2,1,0:T(8,128)(2,1)S(1)} all-to-all(bf16[8,16,1536]{2,1,0:T(8,128)(2,1)S(1)} %bitcast.20), channel_id=1, replica_groups=mesh['z_hi'=4,'z_lo'=3,'x_lo'=2,'expert'=8,'x_hi'=2,'core'=2] {'expert'}, dimensions={0} | all-to-all | bytes 786432 | tf_op jit(solution)/shard_map/all_to_all | solution.py:254
  133.1 0.9 fusion
  (7 shorter events, 0.1 us)
Async XLA Ops:
  1.6 1.0 copy-start.1
  4.0 22.3 %all-to-all-start = ((bf16[6,32,640]{2,1,0:T(8,128)(2,1)}), bf16[6,32,640]{2,1,0:T(8,128)(2,1)S(1)}, u32[]{:S(2)}, u32[]{:S(2)}) async-start(bf16[6,32,640]{2,1,0:T(8,128)(2,1)} %get-tuple-element.16), calls=%async_computation | async-start | bytes 491520 | tf_op jit(solution)/shard_map/all_to_all | solution.py:175
  10.9 1.0 copy-start
  13.8 21.5 %collective-permute-start = (bf16[2,128,512]{2,1,0:T(8,128)(2,1)S(1)}, bf16[2,128,512]{2,1,0:T(8,128)(2,1)S(1)}, u32[]{:S(2)}, u32[]{:S(2)}) collective-permute-start(bf16[2,128,512]{2,1,0:T(8,128)(2,1)S(1)} %sync_rows.1.here), channel_id=1, source_target_pairs={{0,192},{1,577},{192,384},{193,1},{384,576},{385,193},{576,0},{577... | collective-permute-start | bytes 786440 | tf_op jit(solution)/shard_map/ppermute | solution.py:195
  35.2 39.5 %all-to-all-start.1 = ((bf16[8,6,16,512]{3,2,1,0:T(8,128)(2,1)}), bf16[8,6,16,512]{3,2,1,0:T(8,128)(2,1)S(1)}, u32[]{:S(2)}, u32[]{:S(2)}) async-start(bf16[8,6,16,512]{3,2,1,0:T(8,128)(2,1)} %dispatch_rows.1), calls=%async_computation.1 | async-start | bytes 1572864 | tf_op jit(solution)/shard_map/all_to_all | solution.py:211
  44.7 41.6 %collective-permute-start.4 = (bf16[256,3072]{1,0:T(8,128)(2,1)}, bf16[256,3072]{1,0:T(8,128)(2,1)S(1)}, u32[]{:S(2)}, u32[]{:S(2)}) collective-permute-start(bf16[256,3072]{1,0:T(8,128)(2,1)} %dynamic-slice_bitcast_fusion), channel_id=1, source_target_pairs={{0,34},{1,35},{2,32},{3,33},{32,2},{33,3},{34,0},{35,1},{4,38},{5,... | collective-permute-start | bytes 4718600 | tf_op jit(solution)/shard_map/ppermute | solution.py:216
  49.3 14.6 %collective-permute-start.1 = (bf16[2,128,512]{2,1,0:T(8,128)(2,1)S(1)}, bf16[2,128,512]{2,1,0:T(8,128)(2,1)S(1)}, u32[]{:S(2)}, u32[]{:S(2)}) collective-permute-start(bf16[2,128,512]{2,1,0:T(8,128)(2,1)S(1)} %sync_rows.1.here), channel_id=1, source_target_pairs={{0,576},{1,193},{192,0},{193,385},{384,192},{385,577},{576,384},{5... | collective-permute-start | bytes 786440 | tf_op jit(solution)/shard_map/ppermute | solution.py:195
  51.9 22.8 %collective-permute-start.2 = (bf16[2,128,512]{2,1,0:T(8,128)(2,1)S(1)}, bf16[2,128,512]{2,1,0:T(8,128)(2,1)S(1)}, u32[]{:S(2)}, u32[]{:S(2)}) collective-permute-start(bf16[2,128,512]{2,1,0:T(8,128)(2,1)S(1)} %collective-permute-done.first), channel_id=1, source_target_pairs={{0,192},{1,577},{192,384},{193,1},{384,576},{385,193},{576,0},{577... | collective-permute-start | bytes 786440 | tf_op jit(solution)/shard_map/ppermute | solution.py:195
  74.7 4.3 %collective-permute-start.3 = (bf16[768,512]{1,0:T(8,128)(2,1)S(1)}, bf16[768,512]{1,0:T(8,128)(2,1)S(1)}, u32[]{:S(2)}, u32[]{:S(2)}) collective-permute-start(bf16[768,512]{1,0:T(8,128)(2,1)S(1)} %bitcast.18), channel_id=1, source_target_pairs={{0,1},{1,0},{2,3},{3,2},{4,5},{5,4},{6,7},{7,6},{8,9},{9,8},{10,11... | collective-permute-start | bytes 2359304 | tf_op jit(solution)/shard_map/ppermute | solution.py:214
  80.9 18.5 %all-to-all-start.2 = ((bf16[6,128,512]{2,1,0:T(8,128)(2,1)}), bf16[6,128,512]{2,1,0:T(8,128)(2,1)}, u32[]{:S(2)}, u32[]{:S(2)}) async-start(bf16[6,128,512]{2,1,0:T(8,128)(2,1)} %gate_up.1), calls=%async_computation.2 | async-start | bytes 1572864 | tf_op jit(solution)/shard_map/all_to_all | solution.py:238
  87.7 21.4 %collective-permute-start.5 = (bf16[2,256,1536]{2,1,0:T(8,128)(2,1)}, bf16[2,256,1536]{2,1,0:T(8,128)(2,1)S(1)}, u32[]{:S(2)}, u32[]{:S(2)}) collective-permute-start(bf16[2,256,1536]{2,1,0:T(8,128)(2,1)} %pad_maximum_fusion), channel_id=1, source_target_pairs={{0,1},{1,0},{2,3},{3,2},{4,5},{5,4},{6,7},{7,6},{8,9},{9,8},{10,11... | collective-permute-start | bytes 4718600 | tf_op jit(solution)/shard_map/ppermute | solution.py:221

commit v2 on v1

--- a/solution.py
+++ b/solution.py
@@ -123,15 +123,11 @@
             ]
 
 
-def down_kernel(place, hidden, own, crossed, sibling, out):
-    units = own.shape[1]
-    tensor = place[1]
-    total = None
-    for flip, columns in enumerate((own[0], sibling[0], crossed[...], sibling[1])):
-        at = pl.ds(pl.multiple_of((tensor ^ flip) * units, units), units)
-        term = jnp.dot(hidden[:, at], columns, preferred_element_type=jnp.float32)
-        total = term if total is None else total + term
-    out[...] = total.astype(jnp.bfloat16)
+def down_kernel(place, own, other, own_low, own_high, other_low, other_high, out):
+    for side, (mine, theirs) in enumerate(((own_low, other_low), (own_high, other_high))):
+        total = jnp.dot(own[...], mine[0], preferred_element_type=jnp.float32)
+        total += jnp.dot(other[...], theirs[0], preferred_element_type=jnp.float32)
+        out[side] = total.astype(jnp.bfloat16)
 
 
 def shards(tokens, expert_ids, gate_values, rollout_gate_up, learner_gate_up, down_weight):
@@ -213,21 +209,7 @@
     own = arrived.reshape(PARTS * slots, ring * BLOCK)
     other = lax.ppermute(own, "core", [(0, 1), (1, 0)])
 
-    crossed = lax.ppermute(
-        lax.dynamic_slice_in_dim(down_weight[0], (1 - tensor // 2) * 2 * quarter, 2 * quarter, 1),
-        ("x_lo", "x_hi", "core"),
-        [(i, i ^ 6) for i in range(8)],
-    )
-    sibling = lax.ppermute(
-        jnp.stack(
-            [
-                lax.dynamic_slice_in_dim(down_weight[0], (tensor ^ 1) * quarter, quarter, 1),
-                lax.dynamic_slice_in_dim(crossed, (1 - tensor % 2) * quarter, quarter, 1),
-            ]
-        ),
-        "core",
-        [(0, 1), (1, 0)],
-    )
+    down_other = lax.ppermute(down_weight, "core", [(0, 1), (1, 0)])
 
     partial = pl.pallas_call(
         gate_up_kernel,
@@ -238,29 +220,27 @@
     partial = lax.all_to_all(partial, ("z_lo", "x_lo"), split_axis=0, concat_axis=0, tiled=True)
     both = jnp.sum(partial.astype(jnp.float32), axis=0)
     hidden = (jax.nn.silu(both[:, :units]) * both[:, units:]).astype(jnp.bfloat16)
-    hidden = lax.all_gather(hidden, ("x_hi", "core"), axis=1, tiled=True)
+    hidden_other = lax.ppermute(hidden, "core", [(0, 1), (1, 0)])
+    low = pl.BlockSpec((1, units, quarter), lambda i, p: (0, 0, p[0]))
+    high = pl.BlockSpec((1, units, quarter), lambda i, p: (0, 0, 2 + p[0]))
+    sides = tensor_count // 2
     expert_out = call(
         down_kernel,
-        jax.ShapeDtypeStruct((slots, quarter), jnp.bfloat16),
-        [
-            whole(slots, tensor_count * units),
-            pl.BlockSpec((1, units, quarter), lambda i, p: (0, 0, p[1])),
-            pl.BlockSpec((units, quarter), lambda i, p: (0, p[0])),
-            whole(2, units, quarter),
-        ],
-        whole(slots, quarter),
+        jax.ShapeDtypeStruct((sides, slots, quarter), jnp.bfloat16),
+        [whole(slots, units), whole(slots, units), low, high, low, high],
+        whole(sides, slots, quarter),
         "down",
-    )(place, hidden, down_weight, crossed, sibling)
+    )(place, hidden, hidden_other, down_weight, down_weight, down_other, down_other)
     back = lax.all_to_all(
-        expert_out.reshape(expert_count, step_count * CAP, quarter),
-        "expert",
+        expert_out.reshape(sides * expert_count, step_count * CAP, quarter),
+        ("x_hi", "expert"),
         split_axis=0,
         concat_axis=0,
         tiled=True,
     )
     mixed = jnp.dot(
-        combine,
-        back.reshape(slots, quarter).astype(jnp.float32),
+        jnp.concatenate([combine] * sides, axis=1),
+        back.reshape(sides * slots, quarter).astype(jnp.float32),
         precision=lax.Precision.HIGHEST,
     )
     return mixed.astype(jnp.bfloat16).reshape(step_count, token_count, quarter)

time: 135 us -> 137 us (1.015)
  blocking collectives: 30.1 us -> 48.6 us
  waiting for transfers between devices: 34.2 us -> 21.7 us
  starting transfers between devices: 48.7 us -> 44.1 us
  other arithmetic: 2.69 us -> 0.23 us
    all_to_all x1 -> x2, blocking collectives: 21.8 us -> 48.6 us  [the longest x1 30.7 us: shards(): lax.all_to_all(expert_out.reshape(sides * expert_count, step_count * CAP,...]
    all_to_all x1 -> x0, waiting for transfers between devices: 9.46 us -> none  [shards(): lax.all_to_all(partial, ('z_lo', 'x_lo'), split_axis=0, concat_axis=0, ti...]
    all_gather x1 -> x0, blocking collectives: 8.33 us -> none  [shards(): hidden = lax.all_gather(hidden, ('x_hi', 'core'), axis=1, tiled=True)]
    unnamed x4 -> x18, local copies, waits for them, and re-layouts: 2.04 us -> 7.07 us
    all_to_all x1 -> x0, starting transfers between devices: 4.21 us -> none  [shards(): lax.all_to_all(partial, ('z_lo', 'x_lo'), split_axis=0, concat_axis=0, ti...]
    dynamic_slice x2 -> x0, local copies, waits for them, and re-layouts: 3.87 us -> none  [the longest x1 2.68 us: shards(): lax.dynamic_slice_in_dim(down_weight[0], (1 - tensor // 2) * 2 * quarter,...]
    ppermute x3, waiting for transfers between devices: 22.8 us -> 20.7 us  [along(): return lax.ppermute(value, ('z_hi', 'core'), perm)]
    ppermute x1, waiting for transfers between devices: 1.89 us -> 0.16 us  [shards(): other = lax.ppermute(own, 'core', [(0, 1), (1, 0)])]
  transfers between devices with their start and end apart: 9 -> 8, of which waited for: 5 -> 5; matrix products, arithmetic and copies ran while one was open for 5% -> 0% of each run, Pallas kernels for 5% -> 5%
where the time goes in v2:
time: 137 us; the launch traced here: 135 us
  blocking collectives  48.6 us (35%)
  starting transfers between devices  44.1 us (32%)
  waiting for transfers between devices  21.7 us (16%)
  Pallas kernels  10.7 us (8%)
  local copies, waits for them, and re-layouts  8.63 us (6%)
    all_to_all x1, blocking collectives, shards(): lax.all_to_all(expert_out.reshape(sides * expert_count, step_count * CAP,...  30.7 us
    ppermute x3, starting transfers between devices, along(): return lax.ppermute(value, ('z_hi', 'core'), perm)  21.6 us
    ppermute x3, waiting for transfers between devices, along(): return lax.ppermute(value, ('z_hi', 'core'), perm)  20.7 us
    all_to_all x1, blocking collectives, shards(): lax.all_to_all(partial, ('z_lo', 'x_lo'), split_axis=0, concat_axis=0, ti...  17.9 us
    unnamed x18, local copies, waits for them, and re-layouts  7.07 us
    all_to_all x1, starting transfers between devices, shards(): lax.all_to_all(packed, ('z_lo', 'x_lo'), split_axis=0, concat_axis=0, til...  6.93 us
    all_to_all x1, starting transfers between devices, shards(): lax.all_to_all(outgoing, 'expert', split_axis=0, concat_axis=0, tiled=True)  6.82 us
    ppermute x1, starting transfers between devices, shards(): hidden_other = lax.ppermute(hidden, 'core', [(0, 1), (1, 0)])  3.85 us
  transfers between devices with their start and end apart: 8, of which 5 were waited for; matrix products, arithmetic and copies ran while one was open for 0% of the time, Pallas kernels for 5%

profile of v2, /device:TPU:1, one launch (start us, length us, event | category | flops | bytes accessed | tf_op | source)
XLA Modules:
  0.0 135.3 jit_solution(13918232126303904287)
XLA Ops:
  0.0 0.8 copy.11
  0.8 0.8 copy.12
  1.6 1.0 copy-done.3
  2.6 1.3 pack_rows.1
  4.0 6.9 %all-to-all-start = ((bf16[6,32,640]{2,1,0:T(8,128)(2,1)}), bf16[6,32,640]{2,1,0:T(8,128)(2,1)}, u32[]{:S(2)}, u32[]{:S(2)}) async-start(bf16[6,32,640]{2,1,0:T(8,128)(2,1)} %get-tuple-element.16), calls=%async_computation | async-start | bytes 491520 | tf_op jit(solution)/shard_map/all_to_all | solution.py:171
  10.9 1.0 copy-done.2
  11.9 2.1 %sync_rows.1.here = bf16[2,128,512]{2,1,0:T(8,128)(2,1)S(1)} custom-call(s32[4]{0:T(128)S(1)} %pad_add_fusion.place, f32[1,2,256,256]{3,2,1,0:T(8,128)S(1)} %copy-done.2, bf16[1,2,6144,256]{3,2,1,0:T(8,128)(2,1)} %rollout.1), custom_call_target="tpu_custom_call" | custom-call | tf_op jit(solution)/shard_map/sync_rows/pallas_call | solution.py:174
  14.0 12.5 %collective-permute-start = (bf16[2,128,512]{2,1,0:T(8,128)(2,1)S(1)}, bf16[2,128,512]{2,1,0:T(8,128)(2,1)}, u32[]{:S(2)}, u32[]{:S(2)}) collective-permute-start(bf16[2,128,512]{2,1,0:T(8,128)(2,1)S(1)} %sync_rows.1.here), channel_id=1, source_target_pairs={{0,192},{1,577},{192,384},{193,1},{384,576},{385,193},{576,0},{577... | collective-permute-start | bytes 786440 | tf_op jit(solution)/shard_map/ppermute | solution.py:191
  26.6 2.5 %dispatch_rows.1 = bf16[8,6,16,512]{3,2,1,0:T(8,128)(2,1)S(1)} custom-call(bf16[6,32,640]{2,1,0:T(8,128)(2,1)} %all-to-all-done.arrived), custom_call_target="tpu_custom_call" | custom-call | tf_op jit(solution)/shard_map/dispatch_rows/pallas_call | solution.py:197
  29.1 0.9 copy-done.1
  30.0 5.5 %collective-permute-done.first = bf16[2,128,512]{2,1,0:T(8,128)(2,1)} collective-permute-done((bf16[2,128,512]{2,1,0:T(8,128)(2,1)S(1)}, bf16[2,128,512]{2,1,0:T(8,128)(2,1)}, u32[]{:S(2)}, u32[]{:S(2)}) %collective-permute-start) | collective-permute-done | bytes 262176 | tf_op jit(solution)/shard_map/ppermute | solution.py:191
  35.5 6.8 %all-to-all-start.1 = ((bf16[8,6,16,512]{3,2,1,0:T(8,128)(2,1)}), bf16[8,6,16,512]{3,2,1,0:T(8,128)(2,1)}, u32[]{:S(2)}, u32[]{:S(2)}) async-start(bf16[8,6,16,512]{3,2,1,0:T(8,128)(2,1)} %copy-done.1), calls=%async_computation.1 | async-start | bytes 1572864 | tf_op jit(solution)/shard_map/all_to_all | solution.py:207
  42.3 1.9 %collective-permute-start.1 = (bf16[2,128,512]{2,1,0:T(8,128)(2,1)S(1)}, bf16[2,128,512]{2,1,0:T(8,128)(2,1)S(1)}, u32[]{:S(2)}, u32[]{:S(2)}) collective-permute-start(bf16[2,128,512]{2,1,0:T(8,128)(2,1)S(1)} %sync_rows.1.here), channel_id=1, source_target_pairs={{0,576},{1,193},{192,0},{193,385},{384,192},{385,577},{576,384},{5... | collective-permute-start | bytes 786440 | tf_op jit(solution)/shard_map/ppermute | solution.py:191
  44.2 7.2 %collective-permute-start.2 = (bf16[2,128,512]{2,1,0:T(8,128)(2,1)}, bf16[2,128,512]{2,1,0:T(8,128)(2,1)S(1)}, u32[]{:S(2)}, u32[]{:S(2)}) collective-permute-start(bf16[2,128,512]{2,1,0:T(8,128)(2,1)} %collective-permute-done.first), channel_id=1, source_target_pairs={{0,192},{1,577},{192,384},{193,1},{384,576},{385,193},{576,0},{577... | collective-permute-start | bytes 786440 | tf_op jit(solution)/shard_map/ppermute | solution.py:191
  51.5 9.4 %collective-permute-done.1.second = bf16[2,128,512]{2,1,0:T(8,128)(2,1)S(1)} collective-permute-done((bf16[2,128,512]{2,1,0:T(8,128)(2,1)S(1)}, bf16[2,128,512]{2,1,0:T(8,128)(2,1)S(1)}, u32[]{:S(2)}, u32[]{:S(2)}) %collective-permute-start.1) | collective-permute-done | bytes 262176 | tf_op jit(solution)/shard_map/ppermute | solution.py:191
  60.9 0.7 copy-done.4
  61.7 5.7 %collective-permute-done.2.far = bf16[2,128,512]{2,1,0:T(8,128)(2,1)S(1)} collective-permute-done((bf16[2,128,512]{2,1,0:T(8,128)(2,1)}, bf16[2,128,512]{2,1,0:T(8,128)(2,1)S(1)}, u32[]{:S(2)}, u32[]{:S(2)}) %collective-permute-start.2) | collective-permute-done | bytes 262176 | tf_op jit(solution)/shard_map/ppermute | solution.py:191
  67.4 0.7 copy-done.6
  68.1 3.0 %collective-permute-start.3 = (bf16[768,512]{1,0:T(8,128)(2,1)}, bf16[768,512]{1,0:T(8,128)(2,1)S(1)}, u32[]{:S(2)}, u32[]{:S(2)}) collective-permute-start(bf16[768,512]{1,0:T(8,128)(2,1)} %bitcast.7.own), channel_id=1, source_target_pairs={{0,1},{1,0},{2,3},{3,2},{4,5},{5,4},{6,7},{7,6},{8,9},{9,8},{10,11... | collective-permute-start | bytes 2359304 | tf_op jit(solution)/shard_map/ppermute | solution.py:210
  71.1 1.9 %collective-permute-start.5 = (bf16[1,256,6144]{2,1,0:T(8,128)(2,1)S(1)}, bf16[1,256,6144]{2,1,0:T(8,128)(2,1)S(1)}, u32[]{:S(2)}, u32[]{:S(2)}) collective-permute-start(bf16[1,256,6144]{2,1,0:T(8,128)(2,1)S(1)} %copy-done), channel_id=1, source_target_pairs={{0,1},{1,0},{2,3},{3,2},{4,5},{5,4},{6,7},{7,6},{8,9},{9,8},{10,11... | collective-permute-start | bytes 9437192 | tf_op jit(solution)/shard_map/ppermute | solution.py:212
  73.0 0.2 collective-permute-done.3.other
  73.2 0.9 copy-done.5
  74.1 0.9 copy-done.7
  75.1 2.2 %gate_up.1 = bf16[6,128,512]{2,1,0:T(8,128)(2,1)S(1)} custom-call(bf16[768,512]{1,0:T(8,128)(2,1)} %bitcast.7.own, bf16[768,512]{1,0:T(8,128)(2,1)S(1)} %collective-permute-done.3.other, bf16[2,128,512]{2,1,0:T(8,128)(2,1)S(1)} %sync_rows.1.here, bf16[2,128,512]{2,1,0:T(8,128)(2,1)} %collective-permute-done.first, bf16[2,128,512]{2,1,0:T(8,128)(2,1)S(1)} %copy-done.5, ...), custom_call_target="tpu_custom_call" | custom-call | tf_op jit(solution)/shard_map/gate_up/pallas_call | solution.py:214
  77.2 17.9 %all_to_all.20 = bf16[6,128,512]{2,1,0:T(8,128)(2,1)S(1)} all-to-all(bf16[6,128,512]{2,1,0:T(8,128)(2,1)S(1)} %gate_up.1), channel_id=1, replica_groups=mesh['z_hi'=4,'z_lo'=3,'x_lo'=2,'expert'=8,'x_hi'=2,'core'=2] {'z_lo','x..., dimensions={0} | all-to-all | bytes 1572864 | tf_op jit(solution)/shard_map/all_to_all | solution.py:220
  95.1 0.1 convert_reduce_fusion
  95.3 3.8 %collective-permute-start.4 = (bf16[128,256]{1,0:T(8,128)(2,1)S(1)}, bf16[128,256]{1,0:T(8,128)(2,1)S(1)}, u32[]{:S(2)}, u32[]{:S(2)}) collective-permute-start(bf16[128,256]{1,0:T(8,128)(2,1)S(1)} %fusion.1.own), channel_id=1, source_target_pairs={{0,1},{1,0},{2,3},{3,2},{4,5},{5,4},{6,7},{7,6},{8,9},{9,8},{10,11... | collective-permute-start | bytes 196616 | tf_op jit(solution)/shard_map/ppermute | solution.py:223
  99.2 0.9 collective-permute-done.4.other
  100.0 0.8 copy-done.8
  100.8 2.6 %down.1 = bf16[2,128,1536]{2,1,0:T(8,128)(2,1)S(1)} custom-call(s32[4]{0:T(128)S(1)} %pad_add_fusion.place, bf16[128,256]{1,0:T(8,128)(2,1)S(1)} %fusion.1.own, bf16[128,256]{1,0:T(8,128)(2,1)S(1)} %collective-permute-done.4.other, bf16[1,256,6144]{2,1,0:T(8,128)(2,1)S(1)} %copy-done, bf16[1,256,6144]{2,1,0:T(8,128)(2,1)S(1)} %copy-done, ...), custom_call_target="tpu_custom_call" | custom-call | tf_op jit(solution)/shard_map/down/pallas_call | solution.py:227
  103.4 30.7 %all_to_all.21 = bf16[16,16,1536]{2,1,0:T(8,128)(2,1)S(1)} all-to-all(bf16[16,16,1536]{2,1,0:T(8,128)(2,1)S(1)} %bitcast.13), channel_id=1, replica_groups=mesh['z_hi'=4,'z_lo'=3,'x_lo'=2,'expert'=8,'x_hi'=2,'core'=2] {'x_hi','e..., dimensions={0} | all-to-all | bytes 1572864 | tf_op jit(solution)/shard_map/all_to_all | solution.py:234
  134.1 1.1 fusion
  (15 shorter events, 0.1 us)
Async XLA Ops:
  1.6 1.0 copy-start.3
  4.0 22.6 %all-to-all-start = ((bf16[6,32,640]{2,1,0:T(8,128)(2,1)}), bf16[6,32,640]{2,1,0:T(8,128)(2,1)}, u32[]{:S(2)}, u32[]{:S(2)}) async-start(bf16[6,32,640]{2,1,0:T(8,128)(2,1)} %get-tuple-element.16), calls=%async_computation | async-start | bytes 491520 | tf_op jit(solution)/shard_map/all_to_all | solution.py:171
  10.9 1.0 copy-start.2
  11.9 59.1 %copy-start = (bf16[1,256,6144]{2,1,0:T(8,128)(2,1)S(1)}, bf16[1,256,6144]{2,1,0:T(8,128)(2,1)}, u32[]{:S(2)}) copy-start(bf16[1,256,6144]{2,1,0:T(8,128)(2,1)} %own_high.1) | copy-start | bytes 9437188
  14.0 21.5 %collective-permute-start = (bf16[2,128,512]{2,1,0:T(8,128)(2,1)S(1)}, bf16[2,128,512]{2,1,0:T(8,128)(2,1)}, u32[]{:S(2)}, u32[]{:S(2)}) collective-permute-start(bf16[2,128,512]{2,1,0:T(8,128)(2,1)S(1)} %sync_rows.1.here), channel_id=1, source_target_pairs={{0,192},{1,577},{192,384},{193,1},{384,576},{385,193},{576,0},{577... | collective-permute-start | bytes 786440 | tf_op jit(solution)/shard_map/ppermute | solution.py:191
  29.1 0.9 copy-start.1
  35.5 32.6 %all-to-all-start.1 = ((bf16[8,6,16,512]{3,2,1,0:T(8,128)(2,1)}), bf16[8,6,16,512]{3,2,1,0:T(8,128)(2,1)}, u32[]{:S(2)}, u32[]{:S(2)}) async-start(bf16[8,6,16,512]{3,2,1,0:T(8,128)(2,1)} %copy-done.1), calls=%async_computation.1 | async-start | bytes 1572864 | tf_op jit(solution)/shard_map/all_to_all | solution.py:207
  42.3 18.6 %collective-permute-start.1 = (bf16[2,128,512]{2,1,0:T(8,128)(2,1)S(1)}, bf16[2,128,512]{2,1,0:T(8,128)(2,1)S(1)}, u32[]{:S(2)}, u32[]{:S(2)}) collective-permute-start(bf16[2,128,512]{2,1,0:T(8,128)(2,1)S(1)} %sync_rows.1.here), channel_id=1, source_target_pairs={{0,576},{1,193},{192,0},{193,385},{384,192},{385,577},{576,384},{5... | collective-permute-start | bytes 786440 | tf_op jit(solution)/shard_map/ppermute | solution.py:191
  44.2 23.1 %collective-permute-start.2 = (bf16[2,128,512]{2,1,0:T(8,128)(2,1)}, bf16[2,128,512]{2,1,0:T(8,128)(2,1)S(1)}, u32[]{:S(2)}, u32[]{:S(2)}) collective-permute-start(bf16[2,128,512]{2,1,0:T(8,128)(2,1)} %collective-permute-done.first), channel_id=1, source_target_pairs={{0,192},{1,577},{192,384},{193,1},{384,576},{385,193},{576,0},{577... | collective-permute-start | bytes 786440 | tf_op jit(solution)/shard_map/ppermute | solution.py:191
  60.9 0.7 copy-start.4
  67.4 0.7 copy-start.6
  68.1 5.1 %collective-permute-start.3 = (bf16[768,512]{1,0:T(8,128)(2,1)}, bf16[768,512]{1,0:T(8,128)(2,1)S(1)}, u32[]{:S(2)}, u32[]{:S(2)}) collective-permute-start(bf16[768,512]{1,0:T(8,128)(2,1)} %bitcast.7.own), channel_id=1, source_target_pairs={{0,1},{1,0},{2,3},{3,2},{4,5},{5,4},{6,7},{7,6},{8,9},{9,8},{10,11... | collective-permute-start | bytes 2359304 | tf_op jit(solution)/shard_map/ppermute | solution.py:210
  71.1 28.1 %collective-permute-start.5 = (bf16[1,256,6144]{2,1,0:T(8,128)(2,1)S(1)}, bf16[1,256,6144]{2,1,0:T(8,128)(2,1)S(1)}, u32[]{:S(2)}, u32[]{:S(2)}) collective-permute-start(bf16[1,256,6144]{2,1,0:T(8,128)(2,1)S(1)} %copy-done), channel_id=1, source_target_pairs={{0,1},{1,0},{2,3},{3,2},{4,5},{5,4},{6,7},{7,6},{8,9},{9,8},{10,11... | collective-permute-start | bytes 9437192 | tf_op jit(solution)/shard_map/ppermute | solution.py:212
  73.2 0.9 copy-start.5
  74.1 0.9 copy-start.7
  95.3 4.7 %collective-permute-start.4 = (bf16[128,256]{1,0:T(8,128)(2,1)S(1)}, bf16[128,256]{1,0:T(8,128)(2,1)S(1)}, u32[]{:S(2)}, u32[]{:S(2)}) collective-permute-start(bf16[128,256]{1,0:T(8,128)(2,1)S(1)} %fusion.1.own), channel_id=1, source_target_pairs={{0,1},{1,0},{2,3},{3,2},{4,5},{5,4},{6,7},{7,6},{8,9},{9,8},{10,11... | collective-permute-start | bytes 196616 | tf_op jit(solution)/shard_map/ppermute | solution.py:223
  99.2 1.7 %copy-start.8 = (bf16[1,256,6144]{2,1,0:T(8,128)(2,1)}, bf16[1,256,6144]{2,1,0:T(8,128)(2,1)S(1)}, u32[]{:S(2)}) copy-start(bf16[1,256,6144]{2,1,0:T(8,128)(2,1)S(1)} %collective-permute-done.5.other_low.other_high) | copy-start | bytes 9437188

commit v3 on v1

--- a/solution.py
+++ b/solution.py
@@ -9,7 +9,6 @@
 BLOCK = 128
 CAP = 4
 STEP_SLOTS = 16
-ORDER = (0, -1, 1, 2)
 PARTS = 6
 VMEM_BYTES = 48 * 1024 * 1024
 
@@ -57,7 +56,7 @@
 
 def pack_kernel(place, ids, gates, tokens, outgoing, combine):
     core, z_high = place[0], place[3]
-    sign = 1 - 2 * core
+    owners = (z_high, z_high ^ (1 + 2 * core), z_high ^ (3 - 2 * core), z_high ^ 2)
     parts, rows, columns = outgoing.shape
     pieces = columns // BLOCK - 1
     steps = rows // 8
@@ -71,8 +70,7 @@
     tail = jnp.where(lane == 0, first, jnp.where(lane == 1, second, 0.0)).astype(jnp.bfloat16)
     for part in range(parts):
         for piece in range(pieces):
-            owner = lax.rem(z_high + sign * ORDER[piece] + pieces, pieces)
-            start = ((owner * parts + part) * 2 + core) * BLOCK
+            start = ((owners[piece] * parts + part) * 2 + core) * BLOCK
             outgoing[part, :, piece * BLOCK : (piece + 1) * BLOCK] = tokens[
                 :, pl.ds(pl.multiple_of(start, BLOCK), BLOCK)
             ]
@@ -186,16 +184,16 @@
         "sync_rows",
     )(place, learner_gate_up, rollout_gate_up)
 
-    def along(value, sign):
+    def paired(value, turn):
         perm = [
-            (i * 2 + core, (i + sign * (1 - 2 * core)) % ring * 2 + core)
+            (i * 2 + core, (i ^ (1 if core == turn else 3)) * 2 + core)
             for i in range(ring)
             for core in range(2)
         ]
         return lax.ppermute(value, ("z_hi", "core"), perm)
 
-    first = along(synced, 1)
-    second = along(synced, -1)
+    first = paired(synced, 0)
+    second = paired(synced, 1)
 
     synced, shared = lax.optimization_barrier((synced, shared))
     outgoing = pl.pallas_call(
@@ -207,14 +205,15 @@
         name="dispatch_rows",
     )(shared)
     outgoing, first = lax.optimization_barrier((outgoing, first))
-    far = along(first, 1)
+    second, down_later = lax.optimization_barrier((second, down_weight))
+    far = paired(first, 1)
     arrived = lax.all_to_all(outgoing, "expert", split_axis=0, concat_axis=0, tiled=True)
     arrived, second, far = lax.optimization_barrier((arrived, second, far))
     own = arrived.reshape(PARTS * slots, ring * BLOCK)
     other = lax.ppermute(own, "core", [(0, 1), (1, 0)])
 
     crossed = lax.ppermute(
-        lax.dynamic_slice_in_dim(down_weight[0], (1 - tensor // 2) * 2 * quarter, 2 * quarter, 1),
+        lax.dynamic_slice_in_dim(down_later[0], (1 - tensor // 2) * 2 * quarter, 2 * quarter, 1),
         ("x_lo", "x_hi", "core"),
         [(i, i ^ 6) for i in range(8)],
     )

time: 135 us -> 143 us (1.059)
  starting transfers between devices: 48.7 us -> 57.2 us
    ppermute x4, starting transfers between devices: 26.1 us -> 20.8 us  [the longest x3 16.3 us: paired(): return lax.ppermute(value, ('z_hi', 'core'), perm)]
    all_to_all x1, starting transfers between devices: 6.82 us -> 11.8 us  [shards(): lax.all_to_all(outgoing, 'expert', split_axis=0, concat_axis=0, tiled=True)]
    ppermute x1, starting transfers between devices: 2.39 us -> 7.1 us  [shards(): other = lax.ppermute(own, 'core', [(0, 1), (1, 0)])]
    all_to_all x1, waiting for transfers between devices: 9.46 us -> 5.28 us  [shards(): lax.all_to_all(partial, ('z_lo', 'x_lo'), split_axis=0, concat_axis=0, ti...]
    ppermute x1, starting transfers between devices: 2.26 us -> 6.3 us  [shards(): lax.ppermute(jnp.stack([lax.dynamic_slice_in_dim(down_weight[0], (tensor...]
    ppermute x4, waiting for transfers between devices: 22.8 us -> 25.7 us  [the longest x3 25.7 us: paired(): return lax.ppermute(value, ('z_hi', 'core'), perm)]
  transfers between devices with their start and end apart: 9 -> 9, of which waited for: 5 -> 5; matrix products, arithmetic and copies ran while one was open for 5% -> 5% of each run, Pallas kernels for 5% -> 4%
where the time goes in v3:
time: 143 us; the launch traced here: 142 us
  starting transfers between devices  57.2 us (40%)
  waiting for transfers between devices  32.9 us (23%)
  blocking collectives  30.6 us (21%)
  Pallas kernels  9.74 us (7%)
  local copies, waits for them, and re-layouts  7.52 us (5%)
  other arithmetic  2.69 us (2%)
    ppermute x3, waiting for transfers between devices, paired(): return lax.ppermute(value, ('z_hi', 'core'), perm)  25.7 us
    all_to_all x1, blocking collectives, shards(): lax.all_to_all(expert_out.reshape(expert_count, step_count * CAP, quarter...  22.1 us
    ppermute x3, starting transfers between devices, paired(): return lax.ppermute(value, ('z_hi', 'core'), perm)  16.3 us
    all_to_all x1, starting transfers between devices, shards(): lax.all_to_all(outgoing, 'expert', split_axis=0, concat_axis=0, tiled=True)  11.8 us
    all_gather x1, blocking collectives, shards(): hidden = lax.all_gather(hidden, ('x_hi', 'core'), axis=1, tiled=True)  8.45 us
    ppermute x1, starting transfers between devices, shards(): other = lax.ppermute(own, 'core', [(0, 1), (1, 0)])  7.1 us
    all_to_all x1, starting transfers between devices, shards(): lax.all_to_all(packed, ('z_lo', 'x_lo'), split_axis=0, concat_axis=0, til...  6.93 us
    ppermute x1, starting transfers between devices, shards(): lax.ppermute(jnp.stack([lax.dynamic_slice_in_dim(down_weight[0], (tensor...  6.3 us
  transfers between devices with their start and end apart: 9, of which 5 were waited for; matrix products, arithmetic and copies ran while one was open for 5% of the time, Pallas kernels for 4%

profile of v3, /device:TPU:1, one launch (start us, length us, event | category | flops | bytes accessed | tf_op | source)
XLA Modules:
  0.0 141.7 jit_solution(3306237956039310159)
XLA Ops:
  0.0 0.8 copy.11
  0.8 0.8 copy.12
  1.6 0.1 pad_add_fusion.place
  1.6 1.0 copy-done.1
  2.6 1.4 pack_rows.1
  4.0 6.9 %all-to-all-start = ((bf16[6,32,640]{2,1,0:T(8,128)(2,1)}), bf16[6,32,640]{2,1,0:T(8,128)(2,1)S(1)}, u32[]{:S(2)}, u32[]{:S(2)}) async-start(bf16[6,32,640]{2,1,0:T(8,128)(2,1)} %get-tuple-element.18), calls=%async_computation | async-start | bytes 491520 | tf_op jit(solution)/shard_map/all_to_all | solution.py:173
  10.9 1.0 copy-done
  12.0 1.8 %sync_rows.1.here = bf16[2,128,512]{2,1,0:T(8,128)(2,1)S(1)} custom-call(s32[4]{0:T(128)S(1)} %pad_add_fusion.place, f32[1,2,256,256]{3,2,1,0:T(8,128)S(1)} %copy-done, bf16[1,2,6144,256]{3,2,1,0:T(8,128)(2,1)} %rollout.1), custom_call_target="tpu_custom_call" | custom-call | tf_op jit(solution)/shard_map/sync_rows/pallas_call | solution.py:176
  13.8 12.5 %collective-permute-start = (bf16[2,128,512]{2,1,0:T(8,128)(2,1)S(1)}, bf16[2,128,512]{2,1,0:T(8,128)(2,1)S(1)}, u32[]{:S(2)}, u32[]{:S(2)}) collective-permute-start(bf16[2,128,512]{2,1,0:T(8,128)(2,1)S(1)} %sync_rows.1.here), channel_id=1, source_target_pairs={{0,192},{1,577},{192,0},{193,385},{384,576},{385,193},{576,384},{5... | collective-permute-start | bytes 786440 | tf_op jit(solution)/shard_map/ppermute | solution.py:193
  26.3 2.4 %dispatch_rows.1 = bf16[8,6,16,512]{3,2,1,0:T(8,128)(2,1)} custom-call(bf16[6,32,640]{2,1,0:T(8,128)(2,1)S(1)} %all-to-all-done.arrived), custom_call_target="tpu_custom_call" | custom-call | tf_op jit(solution)/shard_map/dispatch_rows/pallas_call | solution.py:199
  28.7 1.5 %collective-permute-done.first = bf16[2,128,512]{2,1,0:T(8,128)(2,1)S(1)} collective-permute-done((bf16[2,128,512]{2,1,0:T(8,128)(2,1)S(1)}, bf16[2,128,512]{2,1,0:T(8,128)(2,1)S(1)}, u32[]{:S(2)}, u32[]{:S(2)}) %collective-permute-start) | collective-permute-done | bytes 262176 | tf_op jit(solution)/shard_map/ppermute | solution.py:193
  30.2 11.8 %all-to-all-start.1 = ((bf16[8,6,16,512]{3,2,1,0:T(8,128)(2,1)}), bf16[8,6,16,512]{3,2,1,0:T(8,128)(2,1)S(1)}, u32[]{:S(2)}, u32[]{:S(2)}) async-start(bf16[8,6,16,512]{3,2,1,0:T(8,128)(2,1)} %dispatch_rows.1), calls=%async_computation.1 | async-start | bytes 1572864 | tf_op jit(solution)/shard_map/all_to_all | solution.py:210
  42.0 1.9 %collective-permute-start.1 = (bf16[2,128,512]{2,1,0:T(8,128)(2,1)S(1)}, bf16[2,128,512]{2,1,0:T(8,128)(2,1)S(1)}, u32[]{:S(2)}, u32[]{:S(2)}) collective-permute-start(bf16[2,128,512]{2,1,0:T(8,128)(2,1)S(1)} %sync_rows.1.here), channel_id=1, source_target_pairs={{0,576},{1,193},{192,384},{193,1},{384,192},{385,577},{576,0},{577... | collective-permute-start | bytes 786440 | tf_op jit(solution)/shard_map/ppermute | solution.py:193
  44.0 11.3 %collective-permute-done.1.second = bf16[2,128,512]{2,1,0:T(8,128)(2,1)S(1)} collective-permute-done((bf16[2,128,512]{2,1,0:T(8,128)(2,1)S(1)}, bf16[2,128,512]{2,1,0:T(8,128)(2,1)S(1)}, u32[]{:S(2)}, u32[]{:S(2)}) %collective-permute-start.1) | collective-permute-done | bytes 262176 | tf_op jit(solution)/shard_map/ppermute | solution.py:193
  55.3 2.7 %dynamic-slice_bitcast_fusion = bf16[256,3072]{1,0:T(8,128)(2,1)} fusion(bf16[1,256,6144]{2,1,0:T(8,128)(2,1)} %own.1, s32[]{:T(128)S(6)} %select_n.28), kind=kLoop, calls=%fused_computation.3 | loop fusion | bytes 3145732 | tf_op jit(solution)/shard_map/dynamic_slice | solution.py:216
  57.9 4.5 %collective-permute-start.4 = (bf16[256,3072]{1,0:T(8,128)(2,1)}, bf16[256,3072]{1,0:T(8,128)(2,1)S(1)}, u32[]{:S(2)}, u32[]{:S(2)}) collective-permute-start(bf16[256,3072]{1,0:T(8,128)(2,1)} %dynamic-slice_bitcast_fusion), channel_id=1, source_target_pairs={{0,34},{1,35},{2,32},{3,33},{32,2},{33,3},{34,0},{35,1},{4,38},{5,... | collective-permute-start | bytes 4718600 | tf_op jit(solution)/shard_map/ppermute | solution.py:215
  62.5 1.9 %collective-permute-start.2 = (bf16[2,128,512]{2,1,0:T(8,128)(2,1)S(1)}, bf16[2,128,512]{2,1,0:T(8,128)(2,1)S(1)}, u32[]{:S(2)}, u32[]{:S(2)}) collective-permute-start(bf16[2,128,512]{2,1,0:T(8,128)(2,1)S(1)} %collective-permute-done.first), channel_id=1, source_target_pairs={{0,576},{1,193},{192,384},{193,1},{384,192},{385,577},{576,0},{577... | collective-permute-start | bytes 786440 | tf_op jit(solution)/shard_map/ppermute | solution.py:193
  64.4 12.9 %collective-permute-done.2.far = bf16[2,128,512]{2,1,0:T(8,128)(2,1)S(1)} collective-permute-done((bf16[2,128,512]{2,1,0:T(8,128)(2,1)S(1)}, bf16[2,128,512]{2,1,0:T(8,128)(2,1)S(1)}, u32[]{:S(2)}, u32[]{:S(2)}) %collective-permute-start.2) | collective-permute-done | bytes 262176 | tf_op jit(solution)/shard_map/ppermute | solution.py:193
  77.3 7.1 %collective-permute-start.3 = (bf16[768,512]{1,0:T(8,128)(2,1)S(1)}, bf16[768,512]{1,0:T(8,128)(2,1)S(1)}, u32[]{:S(2)}, u32[]{:S(2)}) collective-permute-start(bf16[768,512]{1,0:T(8,128)(2,1)S(1)} %bitcast.18), channel_id=1, source_target_pairs={{0,1},{1,0},{2,3},{3,2},{4,5},{5,4},{6,7},{7,6},{8,9},{9,8},{10,11... | collective-permute-start | bytes 2359304 | tf_op jit(solution)/shard_map/ppermute | solution.py:213
  84.4 1.9 %collective-permute-done.3.other = bf16[768,512]{1,0:T(8,128)(2,1)S(1)} collective-permute-done((bf16[768,512]{1,0:T(8,128)(2,1)S(1)}, bf16[768,512]{1,0:T(8,128)(2,1)S(1)}, u32[]{:S(2)}, u32[]{:S(2)}) %collective-permute-start.3) | collective-permute-done | bytes 786464 | tf_op jit(solution)/shard_map/ppermute | solution.py:213
  86.3 1.9 %gate_up.1 = bf16[6,128,512]{2,1,0:T(8,128)(2,1)} custom-call(bf16[768,512]{1,0:T(8,128)(2,1)S(1)} %bitcast.19, bf16[768,512]{1,0:T(8,128)(2,1)S(1)} %collective-permute-done.3.other, bf16[2,128,512]{2,1,0:T(8,128)(2,1)S(1)} %sync_rows.1.here, bf16[2,128,512]{2,1,0:T(8,128)(2,1)S(1)} %collective-permute-done.first, ...), custom_call_target="tpu_custom_call" | custom-call | tf_op jit(solution)/shard_map/gate_up/pallas_call | solution.py:231
  88.2 4.2 %all-to-all-start.2 = ((bf16[6,128,512]{2,1,0:T(8,128)(2,1)}), bf16[6,128,512]{2,1,0:T(8,128)(2,1)}, u32[]{:S(2)}, u32[]{:S(2)}) async-start(bf16[6,128,512]{2,1,0:T(8,128)(2,1)} %gate_up.1), calls=%async_computation.2 | async-start | bytes 1572864 | tf_op jit(solution)/shard_map/all_to_all | solution.py:237
  92.4 1.2 constant_dynamic-slice_fusion
  93.6 0.1 dynamic-slice_bitcast_fusion.1
  93.7 1.3 pad_maximum_fusion
  95.0 6.3 %collective-permute-start.5 = (bf16[2,256,1536]{2,1,0:T(8,128)(2,1)}, bf16[2,256,1536]{2,1,0:T(8,128)(2,1)S(1)}, u32[]{:S(2)}, u32[]{:S(2)}) collective-permute-start(bf16[2,256,1536]{2,1,0:T(8,128)(2,1)} %pad_maximum_fusion), channel_id=1, source_target_pairs={{0,1},{1,0},{2,3},{3,2},{4,5},{5,4},{6,7},{7,6},{8,9},{9,8},{10,11... | collective-permute-start | bytes 4718600 | tf_op jit(solution)/shard_map/ppermute | solution.py:220
  101.3 5.3 %all-to-all-done.2 = bf16[6,128,512]{2,1,0:T(8,128)(2,1)} async-done(((bf16[6,128,512]{2,1,0:T(8,128)(2,1)}), bf16[6,128,512]{2,1,0:T(8,128)(2,1)}, u32[]{:S(2)}, u32[]{:S(2)}) %all-to-all-start.2) | async-done | bytes 786464 | tf_op jit(solution)/shard_map/all_to_all | solution.py:237
  106.6 1.3 convert_reduce_fusion
  107.9 8.5 %all_gather.3.hidden = bf16[128,1024]{1,0:T(8,128)(2,1)S(1)} all-gather(bf16[128,256]{1,0:T(8,128)(2,1)S(1)} %fusion.1), channel_id=1, replica_groups=mesh['z_hi'=4,'z_lo'=3,'x_lo'=2,'expert'=8,'x_hi'=2,'core'=2] {'x_hi','c..., dimensions={1}, use_global_device_ids=true | all-gather | bytes 327680 | tf_op jit(solution)/shard_map/all_gather | solution.py:240
  116.4 2.3 %down.1 = bf16[128,1536]{1,0:T(8,128)(2,1)S(1)} custom-call(s32[4]{0:T(128)S(1)} %pad_add_fusion.place, bf16[128,1024]{1,0:T(8,128)(2,1)S(1)} %all_gather.3.hidden, bf16[1,256,6144]{2,1,0:T(8,128)(2,1)} %own.1, bf16[256,3072]{1,0:T(8,128)(2,1)S(1)} %collective-permute-done.4.crossed, bf16[2,256,1536]{2,1,0:T(8,128)(2,1)S(1)} %collective-permute-done.5.sibling), custom_call_target="tpu_custom_call" | custom-call | tf_op jit(solution)/shard_map/down/pallas_call | solution.py:241
  118.6 22.1 %all_to_all.20 = bf16[8,16,1536]{2,1,0:T(8,128)(2,1)S(1)} all-to-all(bf16[8,16,1536]{2,1,0:T(8,128)(2,1)S(1)} %bitcast.20), channel_id=1, replica_groups=mesh['z_hi'=4,'z_lo'=3,'x_lo'=2,'expert'=8,'x_hi'=2,'core'=2] {'expert'}, dimensions={0} | all-to-all | bytes 786432 | tf_op jit(solution)/shard_map/all_to_all | solution.py:253
  140.8 0.9 fusion
  (7 shorter events, 0.1 us)
Async XLA Ops:
  1.6 1.0 copy-start.1
  4.0 22.3 %all-to-all-start = ((bf16[6,32,640]{2,1,0:T(8,128)(2,1)}), bf16[6,32,640]{2,1,0:T(8,128)(2,1)S(1)}, u32[]{:S(2)}, u32[]{:S(2)}) async-start(bf16[6,32,640]{2,1,0:T(8,128)(2,1)} %get-tuple-element.18), calls=%async_computation | async-start | bytes 491520 | tf_op jit(solution)/shard_map/all_to_all | solution.py:173
  10.9 1.0 copy-start
  13.8 16.4 %collective-permute-start = (bf16[2,128,512]{2,1,0:T(8,128)(2,1)S(1)}, bf16[2,128,512]{2,1,0:T(8,128)(2,1)S(1)}, u32[]{:S(2)}, u32[]{:S(2)}) collective-permute-start(bf16[2,128,512]{2,1,0:T(8,128)(2,1)S(1)} %sync_rows.1.here), channel_id=1, source_target_pairs={{0,192},{1,577},{192,0},{193,385},{384,576},{385,193},{576,384},{5... | collective-permute-start | bytes 786440 | tf_op jit(solution)/shard_map/ppermute | solution.py:193
  30.2 47.1 %all-to-all-start.1 = ((bf16[8,6,16,512]{3,2,1,0:T(8,128)(2,1)}), bf16[8,6,16,512]{3,2,1,0:T(8,128)(2,1)S(1)}, u32[]{:S(2)}, u32[]{:S(2)}) async-start(bf16[8,6,16,512]{3,2,1,0:T(8,128)(2,1)} %dispatch_rows.1), calls=%async_computation.1 | async-start | bytes 1572864 | tf_op jit(solution)/shard_map/all_to_all | solution.py:210
  42.0 13.2 %collective-permute-start.1 = (bf16[2,128,512]{2,1,0:T(8,128)(2,1)S(1)}, bf16[2,128,512]{2,1,0:T(8,128)(2,1)S(1)}, u32[]{:S(2)}, u32[]{:S(2)}) collective-permute-start(bf16[2,128,512]{2,1,0:T(8,128)(2,1)S(1)} %sync_rows.1.here), channel_id=1, source_target_pairs={{0,576},{1,193},{192,384},{193,1},{384,192},{385,577},{576,0},{577... | collective-permute-start | bytes 786440 | tf_op jit(solution)/shard_map/ppermute | solution.py:193
  57.9 35.7 %collective-permute-start.4 = (bf16[256,3072]{1,0:T(8,128)(2,1)}, bf16[256,3072]{1,0:T(8,128)(2,1)S(1)}, u32[]{:S(2)}, u32[]{:S(2)}) collective-permute-start(bf16[256,3072]{1,0:T(8,128)(2,1)} %dynamic-slice_bitcast_fusion), channel_id=1, source_target_pairs={{0,34},{1,35},{2,32},{3,33},{32,2},{33,3},{34,0},{35,1},{4,38},{5,... | collective-permute-start | bytes 4718600 | tf_op jit(solution)/shard_map/ppermute | solution.py:215
  62.5 14.9 %collective-permute-start.2 = (bf16[2,128,512]{2,1,0:T(8,128)(2,1)S(1)}, bf16[2,128,512]{2,1,0:T(8,128)(2,1)S(1)}, u32[]{:S(2)}, u32[]{:S(2)}) collective-permute-start(bf16[2,128,512]{2,1,0:T(8,128)(2,1)S(1)} %collective-permute-done.first), channel_id=1, source_target_pairs={{0,576},{1,193},{192,384},{193,1},{384,192},{385,577},{576,0},{577... | collective-permute-start | bytes 786440 | tf_op jit(solution)/shard_map/ppermute | solution.py:193
  77.3 9.0 %collective-permute-start.3 = (bf16[768,512]{1,0:T(8,128)(2,1)S(1)}, bf16[768,512]{1,0:T(8,128)(2,1)S(1)}, u32[]{:S(2)}, u32[]{:S(2)}) collective-permute-start(bf16[768,512]{1,0:T(8,128)(2,1)S(1)} %bitcast.18), channel_id=1, source_target_pairs={{0,1},{1,0},{2,3},{3,2},{4,5},{5,4},{6,7},{7,6},{8,9},{9,8},{10,11... | collective-permute-start | bytes 2359304 | tf_op jit(solution)/shard_map/ppermute | solution.py:213
  88.2 18.4 %all-to-all-start.2 = ((bf16[6,128,512]{2,1,0:T(8,128)(2,1)}), bf16[6,128,512]{2,1,0:T(8,128)(2,1)}, u32[]{:S(2)}, u32[]{:S(2)}) async-start(bf16[6,128,512]{2,1,0:T(8,128)(2,1)} %gate_up.1), calls=%async_computation.2 | async-start | bytes 1572864 | tf_op jit(solution)/shard_map/all_to_all | solution.py:237
  95.0 21.4 %collective-permute-start.5 = (bf16[2,256,1536]{2,1,0:T(8,128)(2,1)}, bf16[2,256,1536]{2,1,0:T(8,128)(2,1)S(1)}, u32[]{:S(2)}, u32[]{:S(2)}) collective-permute-start(bf16[2,256,1536]{2,1,0:T(8,128)(2,1)} %pad_maximum_fusion), channel_id=1, source_target_pairs={{0,1},{1,0},{2,3},{3,2},{4,5},{5,4},{6,7},{7,6},{8,9},{9,8},{10,11... | collective-permute-start | bytes 4718600 | tf_op jit(solution)/shard_map/ppermute | solution.py:220

commit v4 on v1

--- a/solution.py
+++ b/solution.py
@@ -8,9 +8,8 @@
 
 BLOCK = 128
 CAP = 4
-STEP_SLOTS = 16
+PARTS = 6
 ORDER = (0, -1, 1, 2)
-PARTS = 6
 VMEM_BYTES = 48 * 1024 * 1024
 
 clip_level = 2.0
@@ -36,64 +35,42 @@
                 ).astype(jnp.bfloat16)
 
 
-def slot_choice(first, second, experts, steps):
-    rows = first.shape[0]
-    per_step = rows // steps
-    slots = experts * steps * CAP
-    row = lax.broadcasted_iota(jnp.int32, (rows, slots), 0)
-    slot = lax.broadcasted_iota(jnp.int32, (rows, slots), 1)
-    expert = (slot // (steps * CAP)).astype(jnp.float32)
-    from_first, from_second = first == expert, second == expert
-    named = (from_first | from_second).astype(jnp.float32)
-    later = lax.broadcasted_iota(jnp.int32, (rows, rows), 0)
-    earlier = lax.broadcasted_iota(jnp.int32, (rows, rows), 1)
-    before = (earlier < later) & (earlier // per_step == later // per_step)
-    rank = jnp.dot(
-        before.astype(jnp.bfloat16), named.astype(jnp.bfloat16), preferred_element_type=jnp.float32
-    )
-    here = (slot // CAP % steps == row // per_step) & (rank == (slot % CAP).astype(jnp.float32))
-    return from_first & here, from_second & here
-
-
-def pack_kernel(place, ids, gates, tokens, outgoing, combine):
+def dispatch_kernel(place, ids_row, ids_col, gates_col, tokens, outgoing, combine):
     core, z_high = place[0], place[3]
     sign = 1 - 2 * core
-    parts, rows, columns = outgoing.shape
-    pieces = columns // BLOCK - 1
-    steps = rows // 8
-    experts = combine.shape[1] // (steps * CAP)
-    first, second = ids[:, 0:1].astype(jnp.float32), ids[:, 1:2].astype(jnp.float32)
-    chosen_first, chosen_second = slot_choice(first, second, experts, steps)
-    combine[...] = jnp.where(chosen_first, gates[:, 0:1], 0.0) + jnp.where(
-        chosen_second, gates[:, 1:2], 0.0
-    )
-    lane = lax.broadcasted_iota(jnp.int32, (rows, BLOCK), 1)
-    tail = jnp.where(lane == 0, first, jnp.where(lane == 1, second, 0.0)).astype(jnp.bfloat16)
-    for part in range(parts):
+    pieces = outgoing.shape[3] // BLOCK
+    experts, step_slots = outgoing.shape[1:3]
+    count = ids_row.shape[1]
+    rows = count // 2
+    steps = step_slots // CAP
+    per_step = rows // steps
+    slots = experts * step_slots
+    i_row = lax.broadcasted_iota(jnp.int32, (count, count), 1)
+    i_col = lax.broadcasted_iota(jnp.int32, (count, count), 0)
+    same_step = (i_row % rows) // per_step == (i_col % rows) // per_step
+    same = (ids_row[...] == ids_col[...]) & same_step
+    rank_row = jnp.sum((same & (i_col < i_row)).astype(jnp.float32), axis=0, keepdims=True)
+    rank_col = jnp.sum((same & (i_row < i_col)).astype(jnp.float32), axis=1, keepdims=True)
+    step_row = (lax.broadcasted_iota(jnp.int32, (1, count), 1) % rows) // per_step
+    step_col = (lax.broadcasted_iota(jnp.int32, (count, 1), 0) % rows) // per_step
+    slot_row = ids_row[...] * step_slots + step_row * CAP + rank_row.astype(jnp.int32)
+    slot_col = ids_col[...] * step_slots + step_col * CAP + rank_col.astype(jnp.int32)
+    matches = lax.broadcasted_iota(jnp.int32, (slots, count), 0) == slot_row
+    hot = matches.astype(jnp.float32)
+    select = (hot[:, :rows] + hot[:, rows:]).astype(jnp.bfloat16)
+    weighted = jnp.where(
+        lax.broadcasted_iota(jnp.int32, (count, slots), 1) == slot_col, gates_col[...], 0.0
+    )
+    combine[...] = weighted[:rows] + weighted[rows:]
+    for part in range(PARTS):
         for piece in range(pieces):
             owner = lax.rem(z_high + sign * ORDER[piece] + pieces, pieces)
-            start = ((owner * parts + part) * 2 + core) * BLOCK
-            outgoing[part, :, piece * BLOCK : (piece + 1) * BLOCK] = tokens[
-                :, pl.ds(pl.multiple_of(start, BLOCK), BLOCK)
-            ]
-        outgoing[part, :, pieces * BLOCK :] = tail
-
-
-def dispatch_kernel(arrived, outgoing):
-    experts, parts, step_slots, columns = outgoing.shape
-    steps = step_slots // CAP
-    for part in range(parts):
-        tail = arrived[part, :, columns:].astype(jnp.float32)
-        chosen_first, chosen_second = slot_choice(tail[:, 0:1], tail[:, 1:2], experts, steps)
-        select = (chosen_first | chosen_second).astype(jnp.float32).astype(jnp.bfloat16)
-        moved = lax.dot_general(
-            select,
-            arrived[part, :, :columns],
-            (((0,), (0,)), ((), ())),
-            preferred_element_type=jnp.float32,
-        ).astype(jnp.bfloat16)
-        for expert in range(experts):
-            outgoing[expert, part] = moved[expert * step_slots : (expert + 1) * step_slots]
+            start = ((owner * PARTS + part) * 2 + core) * BLOCK
+            columns = tokens[:, pl.ds(pl.multiple_of(start, BLOCK), BLOCK)]
+            moved = jnp.dot(select, columns, preferred_element_type=jnp.float32)
+            outgoing[part, :, :, piece * BLOCK : (piece + 1) * BLOCK] = moved.astype(
+                jnp.bfloat16
+            ).reshape(experts, step_slots, BLOCK)
 
 
 def gate_up_kernel(own, other, here, first, second, far, out):
@@ -112,15 +89,7 @@
             preferred_element_type=jnp.float32,
         )
         total = term if total is None else total + term
-    partial = total.astype(jnp.bfloat16)
-    parts, slots, _ = out.shape
-    experts = own.shape[0] // (parts * STEP_SLOTS)
-    for expert in range(experts):
-        for part in range(parts):
-            at = (expert * parts + part) * STEP_SLOTS
-            out[part, expert * STEP_SLOTS : (expert + 1) * STEP_SLOTS] = partial[
-                at : at + STEP_SLOTS
-            ]
+    out[...] = total.astype(jnp.bfloat16)
 
 
 def down_kernel(place, hidden, own, crossed, sibling, out):
@@ -160,21 +129,6 @@
             name=name,
         )
 
-    flat_tokens = tokens.reshape(step_count * token_count, width)
-    rows = step_count * token_count
-    packed, combine = call(
-        pack_kernel,
-        [
-            jax.ShapeDtypeStruct((PARTS, rows, (ring + 1) * BLOCK), jnp.bfloat16),
-            jax.ShapeDtypeStruct((rows, slots), jnp.float32),
-        ],
-        [whole(rows, 2), whole(rows, 2), whole(rows, width)],
-        [whole(PARTS, rows, (ring + 1) * BLOCK), whole(rows, slots)],
-        "pack_rows",
-    )(place, expert_ids.reshape(rows, 2), gate_values.reshape(rows, 2), flat_tokens)
-    shared = lax.all_to_all(packed, ("z_lo", "x_lo"), split_axis=0, concat_axis=0, tiled=True)
-
-    packed, learner_gate_up = lax.optimization_barrier((packed, learner_gate_up))
     synced = call(
         sync_kernel,
         jax.ShapeDtypeStruct((2, own_rows // 2, 2 * units), jnp.bfloat16),
@@ -197,24 +151,46 @@
     first = along(synced, 1)
     second = along(synced, -1)
 
-    synced, shared = lax.optimization_barrier((synced, shared))
-    outgoing = pl.pallas_call(
+    synced, expert_ids = lax.optimization_barrier((synced, expert_ids))
+    flat_ids = expert_ids.transpose(2, 0, 1).reshape(-1)
+    flat_gates = gate_values.transpose(2, 0, 1).reshape(-1)
+    flat_tokens = tokens.reshape(step_count * token_count, width)
+    count = flat_ids.shape[0]
+    out_dims = (PARTS, expert_count, step_count * CAP, ring * BLOCK)
+    outgoing, combine = call(
         dispatch_kernel,
-        out_shape=jax.ShapeDtypeStruct(
-            (expert_count, PARTS, step_count * CAP, ring * BLOCK), jnp.bfloat16
-        ),
-        compiler_params=pltpu.CompilerParams(vmem_limit_bytes=VMEM_BYTES),
-        name="dispatch_rows",
-    )(shared)
-    outgoing, first = lax.optimization_barrier((outgoing, first))
+        [
+            jax.ShapeDtypeStruct(out_dims, jnp.bfloat16),
+            jax.ShapeDtypeStruct((count // 2, slots), jnp.float32),
+        ],
+        [whole(1, count), whole(count, 1), whole(count, 1), whole(*flat_tokens.shape)],
+        [whole(*out_dims), whole(count // 2, slots)],
+        "dispatch_rows",
+    )(
+        place,
+        flat_ids.reshape(1, count),
+        flat_ids.reshape(count, 1),
+        flat_gates.reshape(count, 1),
+        flat_tokens,
+    )
+    down_half = lax.dynamic_slice_in_dim(
+        down_weight[0], (1 - tensor // 2) * 2 * quarter, 2 * quarter, 1
+    )
+    outgoing, first, down_half = lax.optimization_barrier((outgoing, first, down_half))
     far = along(first, 1)
-    arrived = lax.all_to_all(outgoing, "expert", split_axis=0, concat_axis=0, tiled=True)
+    arrived = lax.all_to_all(
+        outgoing.reshape(PARTS * expert_count, step_count * CAP, ring * BLOCK),
+        ("z_lo", "x_lo", "expert"),
+        split_axis=0,
+        concat_axis=0,
+        tiled=True,
+    )
     arrived, second, far = lax.optimization_barrier((arrived, second, far))
     own = arrived.reshape(PARTS * slots, ring * BLOCK)
     other = lax.ppermute(own, "core", [(0, 1), (1, 0)])
 
     crossed = lax.ppermute(
-        lax.dynamic_slice_in_dim(down_weight[0], (1 - tensor // 2) * 2 * quarter, 2 * quarter, 1),
+        down_half,
         ("x_lo", "x_hi", "core"),
         [(i, i ^ 6) for i in range(8)],
     )
@@ -231,11 +207,17 @@
 
     partial = pl.pallas_call(
         gate_up_kernel,
-        out_shape=jax.ShapeDtypeStruct((PARTS, slots, 2 * units), jnp.bfloat16),
+        out_shape=jax.ShapeDtypeStruct((PARTS * slots, 2 * units), jnp.bfloat16),
         compiler_params=pltpu.CompilerParams(vmem_limit_bytes=VMEM_BYTES),
         name="gate_up",
     )(own, other, synced, first, second, far)
-    partial = lax.all_to_all(partial, ("z_lo", "x_lo"), split_axis=0, concat_axis=0, tiled=True)
+    partial = lax.all_to_all(
+        partial.reshape(PARTS, slots, 2 * units),
+        ("z_lo", "x_lo"),
+        split_axis=0,
+        concat_axis=0,
+        tiled=True,
+    )
     both = jnp.sum(partial.astype(jnp.float32), axis=0)
     hidden = (jax.nn.silu(both[:, :units]) * both[:, units:]).astype(jnp.bfloat16)
     hidden = lax.all_gather(hidden, ("x_hi", "core"), axis=1, tiled=True)

time: 135 us -> 129 us (0.956)
  waiting for transfers between devices: 34.2 us -> 25.2 us
  starting transfers between devices: 48.7 us -> 55.9 us
  local copies, waits for them, and re-layouts: 7.52 us -> 5.22 us
  Pallas kernels: 9.75 us -> 7.86 us
    ppermute x3, waiting for transfers between devices: 22.8 us -> 14.4 us  [along(): return lax.ppermute(value, ('z_hi', 'core'), perm)]
    ppermute x1, starting transfers between devices: 2.39 us -> 6.18 us  [shards(): other = lax.ppermute(own, 'core', [(0, 1), (1, 0)])]
    ppermute x3, starting transfers between devices: 21.5 us -> 24.2 us  [along(): return lax.ppermute(value, ('z_hi', 'core'), perm)]
    pallas_call x3 -> x2, Pallas kernels: 5.67 us -> 3.78 us  [the longest x1 1.92 us: shards(): call(dispatch_kernel, [jax.ShapeDtypeStruct(out_dims, jnp.bfloat16), jax....]
    reshape x2 -> x0, local copies, waits for them, and re-layouts: 1.56 us -> none  [the longest x1 0.78 us: shards(): expert_ids.reshape(rows, 2)]
    all_to_all x3 -> x2, starting transfers between devices: 18 us -> 18.7 us  [the longest x1 10.3 us: shards(): lax.all_to_all(partial.reshape(PARTS, slots, 2 * units), ('z_lo', 'x_lo')...]
    all_to_all x3 -> x2, waiting for transfers between devices: 9.46 us -> 8.88 us  [the longest x1 8.88 us: shards(): lax.all_to_all(partial.reshape(PARTS, slots, 2 * units), ('z_lo', 'x_lo')...]
  transfers between devices with their start and end apart: 9 -> 8, of which waited for: 5 -> 4; matrix products, arithmetic and copies ran while one was open for 5% -> 5% of each run, Pallas kernels for 5% -> 3%
where the time goes in v4:
time: 129 us; the launch traced here: 128 us
  starting transfers between devices  55.9 us (43%)
  blocking collectives  29.9 us (23%)
  waiting for transfers between devices  25.2 us (20%)
  Pallas kernels  7.86 us (6%)
  local copies, waits for them, and re-layouts  5.22 us (4%)
  other arithmetic  2.69 us (2%)
    ppermute x3, starting transfers between devices, along(): return lax.ppermute(value, ('z_hi', 'core'), perm)  24.2 us
    all_to_all x1, blocking collectives, shards(): lax.all_to_all(expert_out.reshape(expert_count, step_count * CAP, quarter...  21.2 us
    ppermute x3, waiting for transfers between devices, along(): return lax.ppermute(value, ('z_hi', 'core'), perm)  14.4 us
    all_to_all x1, starting transfers between devices, shards(): lax.all_to_all(partial.reshape(PARTS, slots, 2 * units), ('z_lo', 'x_lo')...  10.3 us
    all_to_all x1, waiting for transfers between devices, shards(): lax.all_to_all(partial.reshape(PARTS, slots, 2 * units), ('z_lo', 'x_lo')...  8.88 us
    all_gather x1, blocking collectives, shards(): hidden = lax.all_gather(hidden, ('x_hi', 'core'), axis=1, tiled=True)  8.66 us
    all_to_all x1, starting transfers between devices, shards(): lax.all_to_all(outgoing.reshape(PARTS * expert_count, step_count * CAP, r...  8.46 us
    ppermute x1, starting transfers between devices, shards(): other = lax.ppermute(own, 'core', [(0, 1), (1, 0)])  6.18 us
  transfers between devices with their start and end apart: 8, of which 4 were waited for; matrix products, arithmetic and copies ran while one was open for 5% of the time, Pallas kernels for 3%

profile of v4, /device:TPU:1, one launch (start us, length us, event | category | flops | bytes accessed | tf_op | source)
XLA Modules:
  0.0 127.9 jit_solution(10100494851920725904)
XLA Ops:
  0.0 0.1 pad_add_fusion.place
  0.1 1.0 copy-done
  1.1 1.8 %sync_rows.1.here = bf16[2,128,512]{2,1,0:T(8,128)(2,1)S(1)} custom-call(s32[4]{0:T(128)S(1)} %pad_add_fusion.place, f32[1,2,256,256]{3,2,1,0:T(8,128)S(1)} %copy-done, bf16[1,2,6144,256]{3,2,1,0:T(8,128)(2,1)} %rollout.1), custom_call_target="tpu_custom_call" | custom-call | tf_op jit(solution)/shard_map/sync_rows/pallas_call | solution.py:132
  3.0 15.1 %collective-permute-start = (bf16[2,128,512]{2,1,0:T(8,128)(2,1)S(1)}, bf16[2,128,512]{2,1,0:T(8,128)(2,1)S(1)}, u32[]{:S(2)}, u32[]{:S(2)}) collective-permute-start(bf16[2,128,512]{2,1,0:T(8,128)(2,1)S(1)} %sync_rows.1.here), channel_id=1, source_target_pairs={{0,192},{1,577},{192,384},{193,1},{384,576},{385,193},{576,0},{577... | collective-permute-start | bytes 786440 | tf_op jit(solution)/shard_map/ppermute | solution.py:149
  18.1 0.1 reshape_reshape.9.ids_row
  18.2 0.1 reshape_reshape.12.ids_col
  18.3 0.1 reshape_reshape.13.gates_col
  18.4 1.9 %dispatch_rows.1 = (bf16[6,8,16,512]{3,2,1,0:T(8,128)(2,1)}, f32[32,128]{1,0:T(8,128)S(1)}) custom-call(s32[4]{0:T(128)S(1)} %pad_add_fusion.place, s32[1,64]{1,0:T(1,128)S(1)} %reshape_reshape.9.ids_row, s32[64,1]{1,0:T(8,128)S(1)} %reshape_reshape.12.ids_col, f32[64,1]{1,0:T(8,128)S(1)} %reshape_reshape.13.gates_col, bf16[32,6144]{1,0:T(8,128)(2,1)S(1)} %bitcast.23), custom_call_target="tpu_custom_call" | custom-call | tf_op jit(solution)/shard_map/dispatch_rows/pallas_call | solution.py:160
  20.3 2.7 %dynamic-slice_bitcast_fusion = bf16[256,3072]{1,0:T(8,128)(2,1)} fusion(bf16[1,256,6144]{2,1,0:T(8,128)(2,1)} %own.1, s32[]{:T(128)S(6)} %select_n.28), kind=kLoop, calls=%fused_computation.4 | loop fusion | bytes 3145732 | tf_op jit(solution)/shard_map/dynamic_slice | solution.py:176
  23.0 4.1 %collective-permute-done.first = bf16[2,128,512]{2,1,0:T(8,128)(2,1)S(1)} collective-permute-done((bf16[2,128,512]{2,1,0:T(8,128)(2,1)S(1)}, bf16[2,128,512]{2,1,0:T(8,128)(2,1)S(1)}, u32[]{:S(2)}, u32[]{:S(2)}) %collective-permute-start) | collective-permute-done | bytes 262176 | tf_op jit(solution)/shard_map/ppermute | solution.py:149
  27.0 8.5 %all-to-all-start = ((bf16[48,16,512]{2,1,0:T(8,128)(2,1)}), bf16[48,16,512]{2,1,0:T(8,128)(2,1)S(1)}, u32[]{:S(2)}, u32[]{:S(2)}) async-start(bf16[48,16,512]{2,1,0:T(8,128)(2,1)} %bitcast.8), calls=%async_computation | async-start | bytes 1572864 | tf_op jit(solution)/shard_map/all_to_all | solution.py:181
  35.5 4.3 %collective-permute-start.4 = (bf16[256,3072]{1,0:T(8,128)(2,1)}, bf16[256,3072]{1,0:T(8,128)(2,1)S(1)}, u32[]{:S(2)}, u32[]{:S(2)}) collective-permute-start(bf16[256,3072]{1,0:T(8,128)(2,1)} %dynamic-slice_bitcast_fusion), channel_id=1, source_target_pairs={{0,34},{1,35},{2,32},{3,33},{32,2},{33,3},{34,0},{35,1},{4,38},{5,... | collective-permute-start | bytes 4718600 | tf_op jit(solution)/shard_map/ppermute | solution.py:192
  39.8 3.6 %collective-permute-start.1 = (bf16[2,128,512]{2,1,0:T(8,128)(2,1)S(1)}, bf16[2,128,512]{2,1,0:T(8,128)(2,1)S(1)}, u32[]{:S(2)}, u32[]{:S(2)}) collective-permute-start(bf16[2,128,512]{2,1,0:T(8,128)(2,1)S(1)} %sync_rows.1.here), channel_id=1, source_target_pairs={{0,576},{1,193},{192,0},{193,385},{384,192},{385,577},{576,384},{5... | collective-permute-start | bytes 786440 | tf_op jit(solution)/shard_map/ppermute | solution.py:149
  43.4 5.4 %collective-permute-start.2 = (bf16[2,128,512]{2,1,0:T(8,128)(2,1)S(1)}, bf16[2,128,512]{2,1,0:T(8,128)(2,1)S(1)}, u32[]{:S(2)}, u32[]{:S(2)}) collective-permute-start(bf16[2,128,512]{2,1,0:T(8,128)(2,1)S(1)} %collective-permute-done.first), channel_id=1, source_target_pairs={{0,192},{1,577},{192,384},{193,1},{384,576},{385,193},{576,0},{577... | collective-permute-start | bytes 786440 | tf_op jit(solution)/shard_map/ppermute | solution.py:149
  48.9 10.3 %collective-permute-done.1.second = bf16[2,128,512]{2,1,0:T(8,128)(2,1)S(1)} collective-permute-done((bf16[2,128,512]{2,1,0:T(8,128)(2,1)S(1)}, bf16[2,128,512]{2,1,0:T(8,128)(2,1)S(1)}, u32[]{:S(2)}, u32[]{:S(2)}) %collective-permute-start.1) | collective-permute-done | bytes 262176 | tf_op jit(solution)/shard_map/ppermute | solution.py:149
  59.2 0.0 collective-permute-done.2.far
  59.2 0.0 all-to-all-done
  59.2 6.2 %collective-permute-start.3 = (bf16[768,512]{1,0:T(8,128)(2,1)S(1)}, bf16[768,512]{1,0:T(8,128)(2,1)S(1)}, u32[]{:S(2)}, u32[]{:S(2)}) collective-permute-start(bf16[768,512]{1,0:T(8,128)(2,1)S(1)} %bitcast.20), channel_id=1, source_target_pairs={{0,1},{1,0},{2,3},{3,2},{4,5},{5,4},{6,7},{7,6},{8,9},{9,8},{10,11... | collective-permute-start | bytes 2359304 | tf_op jit(solution)/shard_map/ppermute | solution.py:190
  65.4 1.9 %collective-permute-done.3.other = bf16[768,512]{1,0:T(8,128)(2,1)S(1)} collective-permute-done((bf16[768,512]{1,0:T(8,128)(2,1)S(1)}, bf16[768,512]{1,0:T(8,128)(2,1)S(1)}, u32[]{:S(2)}, u32[]{:S(2)}) %collective-permute-start.3) | collective-permute-done | bytes 786464 | tf_op jit(solution)/shard_map/ppermute | solution.py:190
  67.3 1.9 %gate_up.1 = bf16[768,512]{1,0:T(8,128)(2,1)} custom-call(bf16[768,512]{1,0:T(8,128)(2,1)S(1)} %bitcast.21, bf16[768,512]{1,0:T(8,128)(2,1)S(1)} %collective-permute-done.3.other, bf16[2,128,512]{2,1,0:T(8,128)(2,1)S(1)} %sync_rows.1.here, bf16[2,128,512]{2,1,0:T(8,128)(2,1)S(1)} %collective-permute-done.first, ...), custom_call_target="tpu_custom_call" | custom-call | tf_op jit(solution)/shard_map/gate_up/pallas_call | solution.py:208
  69.2 10.3 %all-to-all-start.1 = ((bf16[6,128,512]{2,1,0:T(8,128)(2,1)}), bf16[6,128,512]{2,1,0:T(8,128)(2,1)}, u32[]{:S(2)}, u32[]{:S(2)}) async-start(bf16[6,128,512]{2,1,0:T(8,128)(2,1)} %bitcast.10), calls=%async_computation.1 | async-start | bytes 1572864 | tf_op jit(solution)/shard_map/all_to_all | solution.py:214
  79.4 1.2 constant_dynamic-slice_fusion
  80.6 0.1 dynamic-slice_bitcast_fusion.1
  80.7 1.3 %pad_maximum_fusion = bf16[2,256,1536]{2,1,0:T(8,128)(2,1)} fusion(bf16[1,256,1536]{2,1,0:T(8,128)(2,1)S(1)} %dynamic-slice_bitcast_fusion.1, bf16[1,256,1536]{2,1,0:T(8,128)(2,1)S(1)} %constant_dynamic-slice_fusion), kind=kLoop, calls=%fused_computation.2 | loop fusion | flops 786432 | bytes 3145728 | tf_op jit(solution)/shard_map/stack | solution.py:198
  82.0 2.6 %collective-permute-start.5 = (bf16[2,256,1536]{2,1,0:T(8,128)(2,1)}, bf16[2,256,1536]{2,1,0:T(8,128)(2,1)S(1)}, u32[]{:S(2)}, u32[]{:S(2)}) collective-permute-start(bf16[2,256,1536]{2,1,0:T(8,128)(2,1)} %pad_maximum_fusion), channel_id=1, source_target_pairs={{0,1},{1,0},{2,3},{3,2},{4,5},{5,4},{6,7},{7,6},{8,9},{9,8},{10,11... | collective-permute-start | bytes 4718600 | tf_op jit(solution)/shard_map/ppermute | solution.py:197
  84.6 8.9 %all-to-all-done.1 = bf16[6,128,512]{2,1,0:T(8,128)(2,1)} async-done(((bf16[6,128,512]{2,1,0:T(8,128)(2,1)}), bf16[6,128,512]{2,1,0:T(8,128)(2,1)}, u32[]{:S(2)}, u32[]{:S(2)}) %all-to-all-start.1) | async-done | bytes 786464 | tf_op jit(solution)/shard_map/all_to_all | solution.py:214
  93.4 1.3 convert_reduce_fusion
  94.8 8.7 %all_gather.3.hidden = bf16[128,1024]{1,0:T(8,128)(2,1)S(1)} all-gather(bf16[128,256]{1,0:T(8,128)(2,1)S(1)} %fusion.1), channel_id=1, replica_groups=mesh['z_hi'=4,'z_lo'=3,'x_lo'=2,'expert'=8,'x_hi'=2,'core'=2] {'x_hi','c..., dimensions={1}, use_global_device_ids=true | all-gather | bytes 327680 | tf_op jit(solution)/shard_map/all_gather | solution.py:223
  103.4 0.0 collective-permute-done.5.sibling
  103.4 2.2 %down.1 = bf16[128,1536]{1,0:T(8,128)(2,1)S(1)} custom-call(s32[4]{0:T(128)S(1)} %pad_add_fusion.place, bf16[128,1024]{1,0:T(8,128)(2,1)S(1)} %all_gather.3.hidden, bf16[1,256,6144]{2,1,0:T(8,128)(2,1)} %own.1, bf16[256,3072]{1,0:T(8,128)(2,1)S(1)} %collective-permute-done.4.crossed, bf16[2,256,1536]{2,1,0:T(8,128)(2,1)S(1)} %collective-permute-done.5.sibling), custom_call_target="tpu_custom_call" | custom-call | tf_op jit(solution)/shard_map/down/pallas_call | solution.py:224
  105.7 21.2 %all_to_all.15 = bf16[8,16,1536]{2,1,0:T(8,128)(2,1)S(1)} all-to-all(bf16[8,16,1536]{2,1,0:T(8,128)(2,1)S(1)} %bitcast.22), channel_id=1, replica_groups=mesh['z_hi'=4,'z_lo'=3,'x_lo'=2,'expert'=8,'x_hi'=2,'core'=2] {'expert'}, dimensions={0} | all-to-all | bytes 786432 | tf_op jit(solution)/shard_map/all_to_all | solution.py:236
  126.9 0.9 fusion
  (11 shorter events, 0.1 us)
Async XLA Ops:
  0.1 1.0 copy-start
  1.1 17.0 %copy-start.2 = (s32[4,8,2]{1,2,0:T(2,128)S(1)}, s32[4,8,2]{1,2,0:T(2,128)}, u32[]{:S(2)}) copy-start(s32[4,8,2]{1,2,0:T(2,128)} %param.7) | copy-start | bytes 772
  1.1 17.2 %copy-start.3 = (f32[4,8,2]{1,2,0:T(2,128)S(1)}, f32[4,8,2]{1,2,0:T(2,128)}, u32[]{:S(2)}) copy-start(f32[4,8,2]{1,2,0:T(2,128)} %param.8) | copy-start | bytes 772
  1.1 17.2 %copy-start.1 = (bf16[4,8,6144]{2,1,0:T(8,128)(2,1)S(1)}, bf16[4,8,6144]{2,1,0:T(8,128)(2,1)}, u32[]{:S(2)}) copy-start(bf16[4,8,6144]{2,1,0:T(8,128)(2,1)} %param.6) | copy-start | bytes 1179652
  3.0 24.1 %collective-permute-start = (bf16[2,128,512]{2,1,0:T(8,128)(2,1)S(1)}, bf16[2,128,512]{2,1,0:T(8,128)(2,1)S(1)}, u32[]{:S(2)}, u32[]{:S(2)}) collective-permute-start(bf16[2,128,512]{2,1,0:T(8,128)(2,1)S(1)} %sync_rows.1.here), channel_id=1, source_target_pairs={{0,192},{1,577},{192,384},{193,1},{384,576},{385,193},{576,0},{577... | collective-permute-start | bytes 786440 | tf_op jit(solution)/shard_map/ppermute | solution.py:149
  27.0 32.2 %all-to-all-start = ((bf16[48,16,512]{2,1,0:T(8,128)(2,1)}), bf16[48,16,512]{2,1,0:T(8,128)(2,1)S(1)}, u32[]{:S(2)}, u32[]{:S(2)}) async-start(bf16[48,16,512]{2,1,0:T(8,128)(2,1)} %bitcast.8), calls=%async_computation | async-start | bytes 1572864 | tf_op jit(solution)/shard_map/all_to_all | solution.py:181
  35.5 45.1 %collective-permute-start.4 = (bf16[256,3072]{1,0:T(8,128)(2,1)}, bf16[256,3072]{1,0:T(8,128)(2,1)S(1)}, u32[]{:S(2)}, u32[]{:S(2)}) collective-permute-start(bf16[256,3072]{1,0:T(8,128)(2,1)} %dynamic-slice_bitcast_fusion), channel_id=1, source_target_pairs={{0,34},{1,35},{2,32},{3,33},{32,2},{33,3},{34,0},{35,1},{4,38},{5,... | collective-permute-start | bytes 4718600 | tf_op jit(solution)/shard_map/ppermute | solution.py:192
  39.8 19.4 %collective-permute-start.1 = (bf16[2,128,512]{2,1,0:T(8,128)(2,1)S(1)}, bf16[2,128,512]{2,1,0:T(8,128)(2,1)S(1)}, u32[]{:S(2)}, u32[]{:S(2)}) collective-permute-start(bf16[2,128,512]{2,1,0:T(8,128)(2,1)S(1)} %sync_rows.1.here), channel_id=1, source_target_pairs={{0,576},{1,193},{192,0},{193,385},{384,192},{385,577},{576,384},{5... | collective-permute-start | bytes 786440 | tf_op jit(solution)/shard_map/ppermute | solution.py:149
  43.4 15.8 %collective-permute-start.2 = (bf16[2,128,512]{2,1,0:T(8,128)(2,1)S(1)}, bf16[2,128,512]{2,1,0:T(8,128)(2,1)S(1)}, u32[]{:S(2)}, u32[]{:S(2)}) collective-permute-start(bf16[2,128,512]{2,1,0:T(8,128)(2,1)S(1)} %collective-permute-done.first), channel_id=1, source_target_pairs={{0,192},{1,577},{192,384},{193,1},{384,576},{385,193},{576,0},{577... | collective-permute-start | bytes 786440 | tf_op jit(solution)/shard_map/ppermute | solution.py:149
  59.2 8.1 %collective-permute-start.3 = (bf16[768,512]{1,0:T(8,128)(2,1)S(1)}, bf16[768,512]{1,0:T(8,128)(2,1)S(1)}, u32[]{:S(2)}, u32[]{:S(2)}) collective-permute-start(bf16[768,512]{1,0:T(8,128)(2,1)S(1)} %bitcast.20), channel_id=1, source_target_pairs={{0,1},{1,0},{2,3},{3,2},{4,5},{5,4},{6,7},{7,6},{8,9},{9,8},{10,11... | collective-permute-start | bytes 2359304 | tf_op jit(solution)/shard_map/ppermute | solution.py:190
  69.2 24.3 %all-to-all-start.1 = ((bf16[6,128,512]{2,1,0:T(8,128)(2,1)}), bf16[6,128,512]{2,1,0:T(8,128)(2,1)}, u32[]{:S(2)}, u32[]{:S(2)}) async-start(bf16[6,128,512]{2,1,0:T(8,128)(2,1)} %bitcast.10), calls=%async_computation.1 | async-start | bytes 1572864 | tf_op jit(solution)/shard_map/all_to_all | solution.py:214
  82.0 21.4 %collective-permute-start.5 = (bf16[2,256,1536]{2,1,0:T(8,128)(2,1)}, bf16[2,256,1536]{2,1,0:T(8,128)(2,1)S(1)}, u32[]{:S(2)}, u32[]{:S(2)}) collective-permute-start(bf16[2,256,1536]{2,1,0:T(8,128)(2,1)} %pad_maximum_fusion), channel_id=1, source_target_pairs={{0,1},{1,0},{2,3},{3,2},{4,5},{5,4},{6,7},{7,6},{8,9},{9,8},{10,11... | collective-permute-start | bytes 4718600 | tf_op jit(solution)/shard_map/ppermute | solution.py:197

commit v5 on v4

--- a/solution.py
+++ b/solution.py
@@ -176,7 +176,9 @@
     down_half = lax.dynamic_slice_in_dim(
         down_weight[0], (1 - tensor // 2) * 2 * quarter, 2 * quarter, 1
     )
-    outgoing, first, down_half = lax.optimization_barrier((outgoing, first, down_half))
+    outgoing, first, second, down_half = lax.optimization_barrier(
+        (outgoing, first, second, down_half)
+    )
     far = along(first, 1)
     arrived = lax.all_to_all(
         outgoing.reshape(PARTS * expert_count, step_count * CAP, ring * BLOCK),
@@ -185,7 +187,7 @@
         concat_axis=0,
         tiled=True,
     )
-    arrived, second, far = lax.optimization_barrier((arrived, second, far))
+    arrived, far = lax.optimization_barrier((arrived, far))
     own = arrived.reshape(PARTS * slots, ring * BLOCK)
     other = lax.ppermute(own, "core", [(0, 1), (1, 0)])
 

time: 129 us -> 131 us (1.016)
    all_to_all x1, starting transfers between devices: 8.46 us -> 15.5 us  [shards(): lax.all_to_all(outgoing.reshape(PARTS * expert_count, step_count * CAP, r...]
    all_to_all x1, waiting for transfers between devices: 0.01 us -> 4.36 us  [shards(): lax.all_to_all(outgoing.reshape(PARTS * expert_count, step_count * CAP, r...]
    ppermute x3, waiting for transfers between devices: 14.4 us -> 10.7 us  [along(): return lax.ppermute(value, ('z_hi', 'core'), perm)]
    all_to_all x1, starting transfers between devices: 10.3 us -> 6.67 us  [shards(): lax.all_to_all(partial.reshape(PARTS, slots, 2 * units), ('z_lo', 'x_lo')...]
    ppermute x1, waiting for transfers between devices: 0.01 us -> 2.05 us  [shards(): lax.ppermute(down_half, ('x_lo', 'x_hi', 'core'), [(i, i ^ 6) for i in ra...]
    ppermute x1, starting transfers between devices: 6.18 us -> 4.42 us  [shards(): other = lax.ppermute(own, 'core', [(0, 1), (1, 0)])]
    all_to_all x1, waiting for transfers between devices: 8.88 us -> 7.5 us  [shards(): lax.all_to_all(partial.reshape(PARTS, slots, 2 * units), ('z_lo', 'x_lo')...]
  transfers between devices with their start and end apart: 8 -> 8, of which waited for: 4 -> 7; matrix products, arithmetic and copies ran while one was open for 5% -> 5% of each run, Pallas kernels for 3% -> 3%
where the time goes in v5:
time: 131 us; the launch traced here: 130 us
  starting transfers between devices  56.4 us (43%)
  blocking collectives  30.1 us (23%)
  waiting for transfers between devices  26.5 us (20%)
  Pallas kernels  7.86 us (6%)
  local copies, waits for them, and re-layouts  5.21 us (4%)
  other arithmetic  2.69 us (2%)
    ppermute x3, starting transfers between devices, along(): return lax.ppermute(value, ('z_hi', 'core'), perm)  23.7 us
    all_to_all x1, blocking collectives, shards(): lax.all_to_all(expert_out.reshape(expert_count, step_count * CAP, quarter...  21.4 us
    all_to_all x1, starting transfers between devices, shards(): lax.all_to_all(outgoing.reshape(PARTS * expert_count, step_count * CAP, r...  15.5 us
    ppermute x3, waiting for transfers between devices, along(): return lax.ppermute(value, ('z_hi', 'core'), perm)  10.7 us
    all_gather x1, blocking collectives, shards(): hidden = lax.all_gather(hidden, ('x_hi', 'core'), axis=1, tiled=True)  8.66 us
    all_to_all x1, waiting for transfers between devices, shards(): lax.all_to_all(partial.reshape(PARTS, slots, 2 * units), ('z_lo', 'x_lo')...  7.5 us
    all_to_all x1, starting transfers between devices, shards(): lax.all_to_all(partial.reshape(PARTS, slots, 2 * units), ('z_lo', 'x_lo')...  6.67 us
    ppermute x1, starting transfers between devices, shards(): other = lax.ppermute(own, 'core', [(0, 1), (1, 0)])  4.42 us
  transfers between devices with their start and end apart: 8, of which 7 were waited for; matrix products, arithmetic and copies ran while one was open for 5% of the time, Pallas kernels for 3%

profile of v5, /device:TPU:1, one launch (start us, length us, event | category | flops | bytes accessed | tf_op | source)
XLA Modules:
  0.0 129.8 jit_solution(6756967401624320118)
XLA Ops:
  0.0 0.1 pad_add_fusion.place
  0.1 1.0 copy-done
  1.1 1.8 %sync_rows.1.here = bf16[2,128,512]{2,1,0:T(8,128)(2,1)S(1)} custom-call(s32[4]{0:T(128)S(1)} %pad_add_fusion.place, f32[1,2,256,256]{3,2,1,0:T(8,128)S(1)} %copy-done, bf16[1,2,6144,256]{3,2,1,0:T(8,128)(2,1)} %rollout.1), custom_call_target="tpu_custom_call" | custom-call | tf_op jit(solution)/shard_map/sync_rows/pallas_call | solution.py:132
  3.0 15.1 %collective-permute-start = (bf16[2,128,512]{2,1,0:T(8,128)(2,1)S(1)}, bf16[2,128,512]{2,1,0:T(8,128)(2,1)S(1)}, u32[]{:S(2)}, u32[]{:S(2)}) collective-permute-start(bf16[2,128,512]{2,1,0:T(8,128)(2,1)S(1)} %sync_rows.1.here), channel_id=1, source_target_pairs={{0,192},{1,577},{192,384},{193,1},{384,576},{385,193},{576,0},{577... | collective-permute-start | bytes 786440 | tf_op jit(solution)/shard_map/ppermute | solution.py:149
  18.1 1.9 %collective-permute-start.1 = (bf16[2,128,512]{2,1,0:T(8,128)(2,1)S(1)}, bf16[2,128,512]{2,1,0:T(8,128)(2,1)S(1)}, u32[]{:S(2)}, u32[]{:S(2)}) collective-permute-start(bf16[2,128,512]{2,1,0:T(8,128)(2,1)S(1)} %sync_rows.1.here), channel_id=1, source_target_pairs={{0,576},{1,193},{192,0},{193,385},{384,192},{385,577},{576,384},{5... | collective-permute-start | bytes 786440 | tf_op jit(solution)/shard_map/ppermute | solution.py:149
  20.0 0.1 reshape_reshape.9.ids_row
  20.1 0.1 reshape_reshape.12.ids_col
  20.2 0.1 reshape_reshape.13.gates_col
  20.3 1.9 %dispatch_rows.1 = (bf16[6,8,16,512]{3,2,1,0:T(8,128)(2,1)}, f32[32,128]{1,0:T(8,128)S(1)}) custom-call(s32[4]{0:T(128)S(1)} %pad_add_fusion.place, s32[1,64]{1,0:T(1,128)S(1)} %reshape_reshape.9.ids_row, s32[64,1]{1,0:T(8,128)S(1)} %reshape_reshape.12.ids_col, f32[64,1]{1,0:T(8,128)S(1)} %reshape_reshape.13.gates_col, bf16[32,6144]{1,0:T(8,128)(2,1)S(1)} %bitcast.23), custom_call_target="tpu_custom_call" | custom-call | tf_op jit(solution)/shard_map/dispatch_rows/pallas_call | solution.py:160
  22.2 2.7 %dynamic-slice_bitcast_fusion = bf16[256,3072]{1,0:T(8,128)(2,1)} fusion(bf16[1,256,6144]{2,1,0:T(8,128)(2,1)} %own.1, s32[]{:T(128)S(6)} %select_n.28), kind=kLoop, calls=%fused_computation.4 | loop fusion | bytes 3145732 | tf_op jit(solution)/shard_map/dynamic_slice | solution.py:176
  24.9 2.0 %collective-permute-done.first = bf16[2,128,512]{2,1,0:T(8,128)(2,1)S(1)} collective-permute-done((bf16[2,128,512]{2,1,0:T(8,128)(2,1)S(1)}, bf16[2,128,512]{2,1,0:T(8,128)(2,1)S(1)}, u32[]{:S(2)}, u32[]{:S(2)}) %collective-permute-start) | collective-permute-done | bytes 262176 | tf_op jit(solution)/shard_map/ppermute | solution.py:149
  26.9 3.8 %collective-permute-done.1.second = bf16[2,128,512]{2,1,0:T(8,128)(2,1)S(1)} collective-permute-done((bf16[2,128,512]{2,1,0:T(8,128)(2,1)S(1)}, bf16[2,128,512]{2,1,0:T(8,128)(2,1)S(1)}, u32[]{:S(2)}, u32[]{:S(2)}) %collective-permute-start.1) | collective-permute-done | bytes 262176 | tf_op jit(solution)/shard_map/ppermute | solution.py:149
  30.6 15.5 %all-to-all-start = ((bf16[48,16,512]{2,1,0:T(8,128)(2,1)}), bf16[48,16,512]{2,1,0:T(8,128)(2,1)S(1)}, u32[]{:S(2)}, u32[]{:S(2)}) async-start(bf16[48,16,512]{2,1,0:T(8,128)(2,1)} %bitcast.8), calls=%async_computation | async-start | bytes 1572864 | tf_op jit(solution)/shard_map/all_to_all | solution.py:183
  46.1 4.3 %collective-permute-start.4 = (bf16[256,3072]{1,0:T(8,128)(2,1)}, bf16[256,3072]{1,0:T(8,128)(2,1)S(1)}, u32[]{:S(2)}, u32[]{:S(2)}) collective-permute-start(bf16[256,3072]{1,0:T(8,128)(2,1)} %dynamic-slice_bitcast_fusion), channel_id=1, source_target_pairs={{0,34},{1,35},{2,32},{3,33},{32,2},{33,3},{34,0},{35,1},{4,38},{5,... | collective-permute-start | bytes 4718600 | tf_op jit(solution)/shard_map/ppermute | solution.py:194
  50.4 6.6 %collective-permute-start.2 = (bf16[2,128,512]{2,1,0:T(8,128)(2,1)S(1)}, bf16[2,128,512]{2,1,0:T(8,128)(2,1)S(1)}, u32[]{:S(2)}, u32[]{:S(2)}) collective-permute-start(bf16[2,128,512]{2,1,0:T(8,128)(2,1)S(1)} %collective-permute-done.first), channel_id=1, source_target_pairs={{0,192},{1,577},{192,384},{193,1},{384,576},{385,193},{576,0},{577... | collective-permute-start | bytes 786440 | tf_op jit(solution)/shard_map/ppermute | solution.py:149
  57.0 5.0 %collective-permute-done.2.far = bf16[2,128,512]{2,1,0:T(8,128)(2,1)S(1)} collective-permute-done((bf16[2,128,512]{2,1,0:T(8,128)(2,1)S(1)}, bf16[2,128,512]{2,1,0:T(8,128)(2,1)S(1)}, u32[]{:S(2)}, u32[]{:S(2)}) %collective-permute-start.2) | collective-permute-done | bytes 262176 | tf_op jit(solution)/shard_map/ppermute | solution.py:149
  62.0 4.4 %all-to-all-done = bf16[48,16,512]{2,1,0:T(8,128)(2,1)S(1)} async-done(((bf16[48,16,512]{2,1,0:T(8,128)(2,1)}), bf16[48,16,512]{2,1,0:T(8,128)(2,1)S(1)}, u32[]{:S(2)}, u32[]{:S(2)}) %all-to-all-start) | async-done | bytes 786464 | tf_op jit(solution)/shard_map/all_to_all | solution.py:183
  66.4 4.4 %collective-permute-start.3 = (bf16[768,512]{1,0:T(8,128)(2,1)S(1)}, bf16[768,512]{1,0:T(8,128)(2,1)S(1)}, u32[]{:S(2)}, u32[]{:S(2)}) collective-permute-start(bf16[768,512]{1,0:T(8,128)(2,1)S(1)} %bitcast.20), channel_id=1, source_target_pairs={{0,1},{1,0},{2,3},{3,2},{4,5},{5,4},{6,7},{7,6},{8,9},{9,8},{10,11... | collective-permute-start | bytes 2359304 | tf_op jit(solution)/shard_map/ppermute | solution.py:192
  70.8 1.9 %collective-permute-done.3.other = bf16[768,512]{1,0:T(8,128)(2,1)S(1)} collective-permute-done((bf16[768,512]{1,0:T(8,128)(2,1)S(1)}, bf16[768,512]{1,0:T(8,128)(2,1)S(1)}, u32[]{:S(2)}, u32[]{:S(2)}) %collective-permute-start.3) | collective-permute-done | bytes 786464 | tf_op jit(solution)/shard_map/ppermute | solution.py:192
  72.7 1.9 %gate_up.1 = bf16[768,512]{1,0:T(8,128)(2,1)} custom-call(bf16[768,512]{1,0:T(8,128)(2,1)S(1)} %bitcast.21, bf16[768,512]{1,0:T(8,128)(2,1)S(1)} %collective-permute-done.3.other, bf16[2,128,512]{2,1,0:T(8,128)(2,1)S(1)} %sync_rows.1.here, bf16[2,128,512]{2,1,0:T(8,128)(2,1)S(1)} %collective-permute-done.first, ...), custom_call_target="tpu_custom_call" | custom-call | tf_op jit(solution)/shard_map/gate_up/pallas_call | solution.py:210
  74.6 6.7 %all-to-all-start.1 = ((bf16[6,128,512]{2,1,0:T(8,128)(2,1)}), bf16[6,128,512]{2,1,0:T(8,128)(2,1)}, u32[]{:S(2)}, u32[]{:S(2)}) async-start(bf16[6,128,512]{2,1,0:T(8,128)(2,1)} %bitcast.10), calls=%async_computation.1 | async-start | bytes 1572864 | tf_op jit(solution)/shard_map/all_to_all | solution.py:216
  81.3 1.2 constant_dynamic-slice_fusion
  82.4 2.1 %collective-permute-done.4.crossed = bf16[256,3072]{1,0:T(8,128)(2,1)S(1)} collective-permute-done((bf16[256,3072]{1,0:T(8,128)(2,1)}, bf16[256,3072]{1,0:T(8,128)(2,1)S(1)}, u32[]{:S(2)}, u32[]{:S(2)}) %collective-permute-start.4) | collective-permute-done | bytes 1572896 | tf_op jit(solution)/shard_map/ppermute | solution.py:194
  84.5 0.1 dynamic-slice_bitcast_fusion.1
  84.5 1.3 %pad_maximum_fusion = bf16[2,256,1536]{2,1,0:T(8,128)(2,1)} fusion(bf16[1,256,1536]{2,1,0:T(8,128)(2,1)S(1)} %dynamic-slice_bitcast_fusion.1, bf16[1,256,1536]{2,1,0:T(8,128)(2,1)S(1)} %constant_dynamic-slice_fusion), kind=kLoop, calls=%fused_computation.2 | loop fusion | flops 786432 | bytes 3145728 | tf_op jit(solution)/shard_map/stack | solution.py:200
  85.9 1.9 %collective-permute-start.5 = (bf16[2,256,1536]{2,1,0:T(8,128)(2,1)}, bf16[2,256,1536]{2,1,0:T(8,128)(2,1)S(1)}, u32[]{:S(2)}, u32[]{:S(2)}) collective-permute-start(bf16[2,256,1536]{2,1,0:T(8,128)(2,1)} %pad_maximum_fusion), channel_id=1, source_target_pairs={{0,1},{1,0},{2,3},{3,2},{4,5},{5,4},{6,7},{7,6},{8,9},{9,8},{10,11... | collective-permute-start | bytes 4718600 | tf_op jit(solution)/shard_map/ppermute | solution.py:199
  87.8 7.5 %all-to-all-done.1 = bf16[6,128,512]{2,1,0:T(8,128)(2,1)} async-done(((bf16[6,128,512]{2,1,0:T(8,128)(2,1)}), bf16[6,128,512]{2,1,0:T(8,128)(2,1)}, u32[]{:S(2)}, u32[]{:S(2)}) %all-to-all-start.1) | async-done | bytes 786464 | tf_op jit(solution)/shard_map/all_to_all | solution.py:216
  95.3 1.3 convert_reduce_fusion
  96.6 8.7 %all_gather.3.hidden = bf16[128,1024]{1,0:T(8,128)(2,1)S(1)} all-gather(bf16[128,256]{1,0:T(8,128)(2,1)S(1)} %fusion.1), channel_id=1, replica_groups=mesh['z_hi'=4,'z_lo'=3,'x_lo'=2,'expert'=8,'x_hi'=2,'core'=2] {'x_hi','c..., dimensions={1}, use_global_device_ids=true | all-gather | bytes 327680 | tf_op jit(solution)/shard_map/all_gather | solution.py:225
  105.3 2.2 %down.1 = bf16[128,1536]{1,0:T(8,128)(2,1)S(1)} custom-call(s32[4]{0:T(128)S(1)} %pad_add_fusion.place, bf16[128,1024]{1,0:T(8,128)(2,1)S(1)} %all_gather.3.hidden, bf16[1,256,6144]{2,1,0:T(8,128)(2,1)} %own.1, bf16[256,3072]{1,0:T(8,128)(2,1)S(1)} %collective-permute-done.4.crossed, bf16[2,256,1536]{2,1,0:T(8,128)(2,1)S(1)} %collective-permute-done.5.sibling), custom_call_target="tpu_custom_call" | custom-call | tf_op jit(solution)/shard_map/down/pallas_call | solution.py:226
  107.5 21.4 %all_to_all.15 = bf16[8,16,1536]{2,1,0:T(8,128)(2,1)S(1)} all-to-all(bf16[8,16,1536]{2,1,0:T(8,128)(2,1)S(1)} %bitcast.22), channel_id=1, replica_groups=mesh['z_hi'=4,'z_lo'=3,'x_lo'=2,'expert'=8,'x_hi'=2,'core'=2] {'expert'}, dimensions={0} | all-to-all | bytes 786432 | tf_op jit(solution)/shard_map/all_to_all | solution.py:238
  128.9 0.9 fusion
  (11 shorter events, 0.1 us)
Async XLA Ops:
  0.1 1.0 copy-start
  1.1 18.9 %copy-start.2 = (s32[4,8,2]{1,2,0:T(2,128)S(1)}, s32[4,8,2]{1,2,0:T(2,128)}, u32[]{:S(2)}) copy-start(s32[4,8,2]{1,2,0:T(2,128)} %param.7) | copy-start | bytes 772
  1.1 19.1 %copy-start.3 = (f32[4,8,2]{1,2,0:T(2,128)S(1)}, f32[4,8,2]{1,2,0:T(2,128)}, u32[]{:S(2)}) copy-start(f32[4,8,2]{1,2,0:T(2,128)} %param.8) | copy-start | bytes 772
  1.1 19.2 %copy-start.1 = (bf16[4,8,6144]{2,1,0:T(8,128)(2,1)S(1)}, bf16[4,8,6144]{2,1,0:T(8,128)(2,1)}, u32[]{:S(2)}) copy-start(bf16[4,8,6144]{2,1,0:T(8,128)(2,1)} %param.6) | copy-start | bytes 1179652
  3.0 23.9 %collective-permute-start = (bf16[2,128,512]{2,1,0:T(8,128)(2,1)S(1)}, bf16[2,128,512]{2,1,0:T(8,128)(2,1)S(1)}, u32[]{:S(2)}, u32[]{:S(2)}) collective-permute-start(bf16[2,128,512]{2,1,0:T(8,128)(2,1)S(1)} %sync_rows.1.here), channel_id=1, source_target_pairs={{0,192},{1,577},{192,384},{193,1},{384,576},{385,193},{576,0},{577... | collective-permute-start | bytes 786440 | tf_op jit(solution)/shard_map/ppermute | solution.py:149
  18.1 12.5 %collective-permute-start.1 = (bf16[2,128,512]{2,1,0:T(8,128)(2,1)S(1)}, bf16[2,128,512]{2,1,0:T(8,128)(2,1)S(1)}, u32[]{:S(2)}, u32[]{:S(2)}) collective-permute-start(bf16[2,128,512]{2,1,0:T(8,128)(2,1)S(1)} %sync_rows.1.here), channel_id=1, source_target_pairs={{0,576},{1,193},{192,0},{193,385},{384,192},{385,577},{576,384},{5... | collective-permute-start | bytes 786440 | tf_op jit(solution)/shard_map/ppermute | solution.py:149
  30.6 35.8 %all-to-all-start = ((bf16[48,16,512]{2,1,0:T(8,128)(2,1)}), bf16[48,16,512]{2,1,0:T(8,128)(2,1)S(1)}, u32[]{:S(2)}, u32[]{:S(2)}) async-start(bf16[48,16,512]{2,1,0:T(8,128)(2,1)} %bitcast.8), calls=%async_computation | async-start | bytes 1572864 | tf_op jit(solution)/shard_map/all_to_all | solution.py:183
  46.1 38.4 %collective-permute-start.4 = (bf16[256,3072]{1,0:T(8,128)(2,1)}, bf16[256,3072]{1,0:T(8,128)(2,1)S(1)}, u32[]{:S(2)}, u32[]{:S(2)}) collective-permute-start(bf16[256,3072]{1,0:T(8,128)(2,1)} %dynamic-slice_bitcast_fusion), channel_id=1, source_target_pairs={{0,34},{1,35},{2,32},{3,33},{32,2},{33,3},{34,0},{35,1},{4,38},{5,... | collective-permute-start | bytes 4718600 | tf_op jit(solution)/shard_map/ppermute | solution.py:194
  50.4 11.7 %collective-permute-start.2 = (bf16[2,128,512]{2,1,0:T(8,128)(2,1)S(1)}, bf16[2,128,512]{2,1,0:T(8,128)(2,1)S(1)}, u32[]{:S(2)}, u32[]{:S(2)}) collective-permute-start(bf16[2,128,512]{2,1,0:T(8,128)(2,1)S(1)} %collective-permute-done.first), channel_id=1, source_target_pairs={{0,192},{1,577},{192,384},{193,1},{384,576},{385,193},{576,0},{577... | collective-permute-start | bytes 786440 | tf_op jit(solution)/shard_map/ppermute | solution.py:149
  66.4 6.3 %collective-permute-start.3 = (bf16[768,512]{1,0:T(8,128)(2,1)S(1)}, bf16[768,512]{1,0:T(8,128)(2,1)S(1)}, u32[]{:S(2)}, u32[]{:S(2)}) collective-permute-start(bf16[768,512]{1,0:T(8,128)(2,1)S(1)} %bitcast.20), channel_id=1, source_target_pairs={{0,1},{1,0},{2,3},{3,2},{4,5},{5,4},{6,7},{7,6},{8,9},{9,8},{10,11... | collective-permute-start | bytes 2359304 | tf_op jit(solution)/shard_map/ppermute | solution.py:192
  74.6 20.7 %all-to-all-start.1 = ((bf16[6,128,512]{2,1,0:T(8,128)(2,1)}), bf16[6,128,512]{2,1,0:T(8,128)(2,1)}, u32[]{:S(2)}, u32[]{:S(2)}) async-start(bf16[6,128,512]{2,1,0:T(8,128)(2,1)} %bitcast.10), calls=%async_computation.1 | async-start | bytes 1572864 | tf_op jit(solution)/shard_map/all_to_all | solution.py:216
  85.9 19.4 %collective-permute-start.5 = (bf16[2,256,1536]{2,1,0:T(8,128)(2,1)}, bf16[2,256,1536]{2,1,0:T(8,128)(2,1)S(1)}, u32[]{:S(2)}, u32[]{:S(2)}) collective-permute-start(bf16[2,256,1536]{2,1,0:T(8,128)(2,1)} %pad_maximum_fusion), channel_id=1, source_target_pairs={{0,1},{1,0},{2,3},{3,2},{4,5},{5,4},{6,7},{7,6},{8,9},{9,8},{10,11... | collective-permute-start | bytes 4718600 | tf_op jit(solution)/shard_map/ppermute | solution.py:199

commit v6 on v4

--- a/solution.py
+++ b/solution.py
@@ -148,7 +148,7 @@
         ]
         return lax.ppermute(value, ("z_hi", "core"), perm)
 
-    first = along(synced, 1)
+    first_low, first_high = along(synced[0], 1), along(synced[1], 1)
     second = along(synced, -1)
 
     synced, expert_ids = lax.optimization_barrier((synced, expert_ids))
@@ -176,7 +176,8 @@
     down_half = lax.dynamic_slice_in_dim(
         down_weight[0], (1 - tensor // 2) * 2 * quarter, 2 * quarter, 1
     )
-    outgoing, first, down_half = lax.optimization_barrier((outgoing, first, down_half))
+    outgoing, first_low, down_half = lax.optimization_barrier((outgoing, first_low, down_half))
+    first = jnp.stack([first_low, first_high])
     far = along(first, 1)
     arrived = lax.all_to_all(
         outgoing.reshape(PARTS * expert_count, step_count * CAP, ring * BLOCK),

time: 129 us -> 131 us (1.016)
  starting transfers between devices: 55.9 us -> 64.6 us
  waiting for transfers between devices: 25.2 us -> 18.7 us
    ppermute x3 -> x4, waiting for transfers between devices: 14.4 us -> 7.89 us  [along(): return lax.ppermute(value, ('z_hi', 'core'), perm)]
    ppermute x1, starting transfers between devices: 6.18 us -> 10.7 us  [shards(): other = lax.ppermute(own, 'core', [(0, 1), (1, 0)])]
    ppermute x3 -> x4, starting transfers between devices: 24.2 us -> 28.4 us  [along(): return lax.ppermute(value, ('z_hi', 'core'), perm)]
    all_to_all x1, starting transfers between devices: 10.3 us -> 8.44 us  [shards(): lax.all_to_all(partial.reshape(PARTS, slots, 2 * units), ('z_lo', 'x_lo')...]
    all_to_all x1, starting transfers between devices: 8.46 us -> 10.3 us  [shards(): lax.all_to_all(outgoing.reshape(PARTS * expert_count, step_count * CAP, r...]
  transfers between devices with their start and end apart: 8 -> 9, of which waited for: 4 -> 4; matrix products, arithmetic and copies ran while one was open for 5% -> 5% of each run, Pallas kernels for 3% -> 3%
where the time goes in v6:
time: 131 us; the launch traced here: 130 us
  starting transfers between devices  64.6 us (49%)
  blocking collectives  30.1 us (23%)
  waiting for transfers between devices  18.7 us (14%)
  Pallas kernels  7.86 us (6%)
  local copies, waits for them, and re-layouts  5.31 us (4%)
  other arithmetic  2.73 us (2%)
    ppermute x4, starting transfers between devices, along(): return lax.ppermute(value, ('z_hi', 'core'), perm)  28.4 us
    all_to_all x1, blocking collectives, shards(): lax.all_to_all(expert_out.reshape(expert_count, step_count * CAP, quarter...  21.4 us
    ppermute x1, starting transfers between devices, shards(): other = lax.ppermute(own, 'core', [(0, 1), (1, 0)])  10.7 us
    all_to_all x1, starting transfers between devices, shards(): lax.all_to_all(outgoing.reshape(PARTS * expert_count, step_count * CAP, r...  10.3 us
    all_to_all x1, waiting for transfers between devices, shards(): lax.all_to_all(partial.reshape(PARTS, slots, 2 * units), ('z_lo', 'x_lo')...  8.9 us
    all_gather x1, blocking collectives, shards(): hidden = lax.all_gather(hidden, ('x_hi', 'core'), axis=1, tiled=True)  8.65 us
    all_to_all x1, starting transfers between devices, shards(): lax.all_to_all(partial.reshape(PARTS, slots, 2 * units), ('z_lo', 'x_lo')...  8.44 us
    ppermute x4, waiting for transfers between devices, along(): return lax.ppermute(value, ('z_hi', 'core'), perm)  7.89 us
  transfers between devices with their start and end apart: 9, of which 4 were waited for; matrix products, arithmetic and copies ran while one was open for 5% of the time, Pallas kernels for 3%

profile of v6, /device:TPU:1, one launch (start us, length us, event | category | flops | bytes accessed | tf_op | source)
XLA Modules:
  0.0 130.4 jit_solution(10464118493654959343)
XLA Ops:
  0.0 0.1 pad_add_fusion.place
  0.1 1.0 copy-done
  1.1 1.8 %sync_rows.1.here = bf16[2,128,512]{2,1,0:T(8,128)(2,1)S(1)} custom-call(s32[4]{0:T(128)S(1)} %pad_add_fusion.place, f32[1,2,256,256]{3,2,1,0:T(8,128)S(1)} %copy-done, bf16[1,2,6144,256]{3,2,1,0:T(8,128)(2,1)} %rollout.1), custom_call_target="tpu_custom_call" | custom-call | tf_op jit(solution)/shard_map/sync_rows/pallas_call | solution.py:132
  3.0 15.1 %collective-permute-start = (bf16[128,512]{1,0:T(8,128)(2,1)S(1)}, bf16[128,512]{1,0:T(8,128)(2,1)S(1)}, u32[]{:S(2)}, u32[]{:S(2)}) collective-permute-start(bf16[128,512]{1,0:T(8,128)(2,1)S(1)} %get-tuple-element.26), channel_id=1, source_target_pairs={{0,192},{1,577},{192,384},{193,1},{384,576},{385,193},{576,0},{577... | collective-permute-start | bytes 393224 | tf_op jit(solution)/shard_map/ppermute | solution.py:149
  18.1 0.0 copy-start.2
  18.1 0.0 copy-start.3
  18.2 2.7 %dynamic-slice_bitcast_fusion = bf16[256,3072]{1,0:T(8,128)(2,1)} fusion(bf16[1,256,6144]{2,1,0:T(8,128)(2,1)} %own.1, s32[]{:T(128)S(6)} %select_n.28), kind=kLoop, calls=%fused_computation.4 | loop fusion | bytes 3145732 | tf_op jit(solution)/shard_map/dynamic_slice | solution.py:176
  20.9 0.1 reshape_reshape.9.ids_row
  21.0 0.1 reshape_reshape.12.ids_col
  21.1 0.1 reshape_reshape.13.gates_col
  21.2 1.9 %dispatch_rows.1 = (bf16[6,8,16,512]{3,2,1,0:T(8,128)(2,1)}, f32[32,128]{1,0:T(8,128)S(1)}) custom-call(s32[4]{0:T(128)S(1)} %pad_add_fusion.place, s32[1,64]{1,0:T(1,128)S(1)} %reshape_reshape.9.ids_row, s32[64,1]{1,0:T(8,128)S(1)} %reshape_reshape.12.ids_col, f32[64,1]{1,0:T(8,128)S(1)} %reshape_reshape.13.gates_col, bf16[32,6144]{1,0:T(8,128)(2,1)S(1)} %bitcast.29), custom_call_target="tpu_custom_call" | custom-call | tf_op jit(solution)/shard_map/dispatch_rows/pallas_call | solution.py:160
  23.1 10.3 %all-to-all-start = ((bf16[48,16,512]{2,1,0:T(8,128)(2,1)}), bf16[48,16,512]{2,1,0:T(8,128)(2,1)S(1)}, u32[]{:S(2)}, u32[]{:S(2)}) async-start(bf16[48,16,512]{2,1,0:T(8,128)(2,1)} %bitcast.9), calls=%async_computation | async-start | bytes 1572864 | tf_op jit(solution)/shard_map/all_to_all | solution.py:182
  33.4 5.0 %collective-permute-start.2 = (bf16[128,512]{1,0:T(8,128)(2,1)S(1)}, bf16[128,512]{1,0:T(8,128)(2,1)S(1)}, u32[]{:S(2)}, u32[]{:S(2)}) collective-permute-start(bf16[128,512]{1,0:T(8,128)(2,1)S(1)} %get-tuple-element.25), channel_id=1, source_target_pairs={{0,192},{1,577},{192,384},{193,1},{384,576},{385,193},{576,0},{577... | collective-permute-start | bytes 393224 | tf_op jit(solution)/shard_map/ppermute | solution.py:149
  38.4 4.3 %collective-permute-start.5 = (bf16[256,3072]{1,0:T(8,128)(2,1)}, bf16[256,3072]{1,0:T(8,128)(2,1)S(1)}, u32[]{:S(2)}, u32[]{:S(2)}) collective-permute-start(bf16[256,3072]{1,0:T(8,128)(2,1)} %dynamic-slice_bitcast_fusion), channel_id=1, source_target_pairs={{0,34},{1,35},{2,32},{3,33},{32,2},{33,3},{34,0},{35,1},{4,38},{5,... | collective-permute-start | bytes 4718600 | tf_op jit(solution)/shard_map/ppermute | solution.py:193
  42.7 2.1 %collective-permute-start.1 = (bf16[2,128,512]{2,1,0:T(8,128)(2,1)S(1)}, bf16[2,128,512]{2,1,0:T(8,128)(2,1)S(1)}, u32[]{:S(2)}, u32[]{:S(2)}) collective-permute-start(bf16[2,128,512]{2,1,0:T(8,128)(2,1)S(1)} %sync_rows.1.here), channel_id=1, source_target_pairs={{0,576},{1,193},{192,0},{193,385},{384,192},{385,577},{576,384},{5... | collective-permute-start | bytes 786440 | tf_op jit(solution)/shard_map/ppermute | solution.py:149
  44.8 6.2 %collective-permute-start.3 = (bf16[2,128,512]{2,1,0:T(8,128)(2,1)S(1)}, bf16[2,128,512]{2,1,0:T(8,128)(2,1)S(1)}, u32[]{:S(2)}, u32[]{:S(2)}) collective-permute-start(bf16[2,128,512]{2,1,0:T(8,128)(2,1)S(1)} %pad_maximum_fusion.1.first), channel_id=1, source_target_pairs={{0,192},{1,577},{192,384},{193,1},{384,576},{385,193},{576,0},{577... | collective-permute-start | bytes 786440 | tf_op jit(solution)/shard_map/ppermute | solution.py:149
  51.0 4.7 %collective-permute-done.1.second = bf16[2,128,512]{2,1,0:T(8,128)(2,1)S(1)} collective-permute-done((bf16[2,128,512]{2,1,0:T(8,128)(2,1)S(1)}, bf16[2,128,512]{2,1,0:T(8,128)(2,1)S(1)}, u32[]{:S(2)}, u32[]{:S(2)}) %collective-permute-start.1) | collective-permute-done | bytes 262176 | tf_op jit(solution)/shard_map/ppermute | solution.py:149
  55.7 3.2 %collective-permute-done.3.far = bf16[2,128,512]{2,1,0:T(8,128)(2,1)S(1)} collective-permute-done((bf16[2,128,512]{2,1,0:T(8,128)(2,1)S(1)}, bf16[2,128,512]{2,1,0:T(8,128)(2,1)S(1)}, u32[]{:S(2)}, u32[]{:S(2)}) %collective-permute-start.3) | collective-permute-done | bytes 262176 | tf_op jit(solution)/shard_map/ppermute | solution.py:149
  58.9 10.7 %collective-permute-start.4 = (bf16[768,512]{1,0:T(8,128)(2,1)S(1)}, bf16[768,512]{1,0:T(8,128)(2,1)S(1)}, u32[]{:S(2)}, u32[]{:S(2)}) collective-permute-start(bf16[768,512]{1,0:T(8,128)(2,1)S(1)} %bitcast.26), channel_id=1, source_target_pairs={{0,1},{1,0},{2,3},{3,2},{4,5},{5,4},{6,7},{7,6},{8,9},{9,8},{10,11... | collective-permute-start | bytes 2359304 | tf_op jit(solution)/shard_map/ppermute | solution.py:191
  69.6 1.9 %collective-permute-done.4.other = bf16[768,512]{1,0:T(8,128)(2,1)S(1)} collective-permute-done((bf16[768,512]{1,0:T(8,128)(2,1)S(1)}, bf16[768,512]{1,0:T(8,128)(2,1)S(1)}, u32[]{:S(2)}, u32[]{:S(2)}) %collective-permute-start.4) | collective-permute-done | bytes 786464 | tf_op jit(solution)/shard_map/ppermute | solution.py:191
  71.5 1.9 %gate_up.1 = bf16[768,512]{1,0:T(8,128)(2,1)} custom-call(bf16[768,512]{1,0:T(8,128)(2,1)S(1)} %bitcast.27, bf16[768,512]{1,0:T(8,128)(2,1)S(1)} %collective-permute-done.4.other, bf16[2,128,512]{2,1,0:T(8,128)(2,1)S(1)} %sync_rows.1.here, bf16[2,128,512]{2,1,0:T(8,128)(2,1)S(1)} %pad_maximum_fusion.1.first, ...), custom_call_target="tpu_custom_call" | custom-call | tf_op jit(solution)/shard_map/gate_up/pallas_call | solution.py:209
  73.3 8.4 %all-to-all-start.1 = ((bf16[6,128,512]{2,1,0:T(8,128)(2,1)}), bf16[6,128,512]{2,1,0:T(8,128)(2,1)}, u32[]{:S(2)}, u32[]{:S(2)}) async-start(bf16[6,128,512]{2,1,0:T(8,128)(2,1)} %bitcast.14), calls=%async_computation.1 | async-start | bytes 1572864 | tf_op jit(solution)/shard_map/all_to_all | solution.py:215
  81.8 1.2 constant_dynamic-slice_fusion
  83.0 0.1 dynamic-slice_bitcast_fusion.1
  83.0 1.3 %pad_maximum_fusion = bf16[2,256,1536]{2,1,0:T(8,128)(2,1)} fusion(bf16[1,256,1536]{2,1,0:T(8,128)(2,1)S(1)} %dynamic-slice_bitcast_fusion.1, bf16[1,256,1536]{2,1,0:T(8,128)(2,1)S(1)} %constant_dynamic-slice_fusion), kind=kLoop, calls=%fused_computation.2 | loop fusion | flops 786432 | bytes 3145728 | tf_op jit(solution)/shard_map/stack | solution.py:199
  84.4 2.5 %collective-permute-start.6 = (bf16[2,256,1536]{2,1,0:T(8,128)(2,1)}, bf16[2,256,1536]{2,1,0:T(8,128)(2,1)S(1)}, u32[]{:S(2)}, u32[]{:S(2)}) collective-permute-start(bf16[2,256,1536]{2,1,0:T(8,128)(2,1)} %pad_maximum_fusion), channel_id=1, source_target_pairs={{0,1},{1,0},{2,3},{3,2},{4,5},{5,4},{6,7},{7,6},{8,9},{9,8},{10,11... | collective-permute-start | bytes 4718600 | tf_op jit(solution)/shard_map/ppermute | solution.py:198
  86.9 8.9 %all-to-all-done.1 = bf16[6,128,512]{2,1,0:T(8,128)(2,1)} async-done(((bf16[6,128,512]{2,1,0:T(8,128)(2,1)}), bf16[6,128,512]{2,1,0:T(8,128)(2,1)}, u32[]{:S(2)}, u32[]{:S(2)}) %all-to-all-start.1) | async-done | bytes 786464 | tf_op jit(solution)/shard_map/all_to_all | solution.py:215
  95.8 1.3 convert_reduce_fusion
  97.1 8.6 %all_gather.3.hidden = bf16[128,1024]{1,0:T(8,128)(2,1)S(1)} all-gather(bf16[128,256]{1,0:T(8,128)(2,1)S(1)} %fusion.1), channel_id=1, replica_groups=mesh['z_hi'=4,'z_lo'=3,'x_lo'=2,'expert'=8,'x_hi'=2,'core'=2] {'x_hi','c..., dimensions={1}, use_global_device_ids=true | all-gather | bytes 327680 | tf_op jit(solution)/shard_map/all_gather | solution.py:224
  105.8 2.2 %down.1 = bf16[128,1536]{1,0:T(8,128)(2,1)S(1)} custom-call(s32[4]{0:T(128)S(1)} %pad_add_fusion.place, bf16[128,1024]{1,0:T(8,128)(2,1)S(1)} %all_gather.3.hidden, bf16[1,256,6144]{2,1,0:T(8,128)(2,1)} %own.1, bf16[256,3072]{1,0:T(8,128)(2,1)S(1)} %collective-permute-done.5.crossed, bf16[2,256,1536]{2,1,0:T(8,128)(2,1)S(1)} %collective-permute-done.6.sibling), custom_call_target="tpu_custom_call" | custom-call | tf_op jit(solution)/shard_map/down/pallas_call | solution.py:225
  108.0 21.4 %all_to_all.15 = bf16[8,16,1536]{2,1,0:T(8,128)(2,1)S(1)} all-to-all(bf16[8,16,1536]{2,1,0:T(8,128)(2,1)S(1)} %bitcast.28), channel_id=1, replica_groups=mesh['z_hi'=4,'z_lo'=3,'x_lo'=2,'expert'=8,'x_hi'=2,'core'=2] {'expert'}, dimensions={0} | all-to-all | bytes 786432 | tf_op jit(solution)/shard_map/all_to_all | solution.py:237
  129.5 0.9 fusion
  (15 shorter events, 0.1 us)
Async XLA Ops:
  0.1 1.0 copy-start
  3.0 20.1 %collective-permute-start = (bf16[128,512]{1,0:T(8,128)(2,1)S(1)}, bf16[128,512]{1,0:T(8,128)(2,1)S(1)}, u32[]{:S(2)}, u32[]{:S(2)}) collective-permute-start(bf16[128,512]{1,0:T(8,128)(2,1)S(1)} %get-tuple-element.26), channel_id=1, source_target_pairs={{0,192},{1,577},{192,384},{193,1},{384,576},{385,193},{576,0},{577... | collective-permute-start | bytes 393224 | tf_op jit(solution)/shard_map/ppermute | solution.py:149
  18.1 2.8 %copy-start.2 = (s32[4,8,2]{1,2,0:T(2,128)S(1)}, s32[4,8,2]{1,2,0:T(2,128)}, u32[]{:S(2)}) copy-start(s32[4,8,2]{1,2,0:T(2,128)} %param.7) | copy-start | bytes 772
  18.1 2.9 %copy-start.3 = (f32[4,8,2]{1,2,0:T(2,128)S(1)}, f32[4,8,2]{1,2,0:T(2,128)}, u32[]{:S(2)}) copy-start(f32[4,8,2]{1,2,0:T(2,128)} %param.8) | copy-start | bytes 772
  18.1 3.0 %copy-start.1 = (bf16[4,8,6144]{2,1,0:T(8,128)(2,1)S(1)}, bf16[4,8,6144]{2,1,0:T(8,128)(2,1)}, u32[]{:S(2)}) copy-start(bf16[4,8,6144]{2,1,0:T(8,128)(2,1)} %param.6) | copy-start | bytes 1179652
  23.1 35.8 %all-to-all-start = ((bf16[48,16,512]{2,1,0:T(8,128)(2,1)}), bf16[48,16,512]{2,1,0:T(8,128)(2,1)S(1)}, u32[]{:S(2)}, u32[]{:S(2)}) async-start(bf16[48,16,512]{2,1,0:T(8,128)(2,1)} %bitcast.9), calls=%async_computation | async-start | bytes 1572864 | tf_op jit(solution)/shard_map/all_to_all | solution.py:182
  33.4 11.4 %collective-permute-start.2 = (bf16[128,512]{1,0:T(8,128)(2,1)S(1)}, bf16[128,512]{1,0:T(8,128)(2,1)S(1)}, u32[]{:S(2)}, u32[]{:S(2)}) collective-permute-start(bf16[128,512]{1,0:T(8,128)(2,1)S(1)} %get-tuple-element.25), channel_id=1, source_target_pairs={{0,192},{1,577},{192,384},{193,1},{384,576},{385,193},{576,0},{577... | collective-permute-start | bytes 393224 | tf_op jit(solution)/shard_map/ppermute | solution.py:149
  38.4 44.6 %collective-permute-start.5 = (bf16[256,3072]{1,0:T(8,128)(2,1)}, bf16[256,3072]{1,0:T(8,128)(2,1)S(1)}, u32[]{:S(2)}, u32[]{:S(2)}) collective-permute-start(bf16[256,3072]{1,0:T(8,128)(2,1)} %dynamic-slice_bitcast_fusion), channel_id=1, source_target_pairs={{0,34},{1,35},{2,32},{3,33},{32,2},{33,3},{34,0},{35,1},{4,38},{5,... | collective-permute-start | bytes 4718600 | tf_op jit(solution)/shard_map/ppermute | solution.py:193
  42.7 13.0 %collective-permute-start.1 = (bf16[2,128,512]{2,1,0:T(8,128)(2,1)S(1)}, bf16[2,128,512]{2,1,0:T(8,128)(2,1)S(1)}, u32[]{:S(2)}, u32[]{:S(2)}) collective-permute-start(bf16[2,128,512]{2,1,0:T(8,128)(2,1)S(1)} %sync_rows.1.here), channel_id=1, source_target_pairs={{0,576},{1,193},{192,0},{193,385},{384,192},{385,577},{576,384},{5... | collective-permute-start | bytes 786440 | tf_op jit(solution)/shard_map/ppermute | solution.py:149
  44.8 14.1 %collective-permute-start.3 = (bf16[2,128,512]{2,1,0:T(8,128)(2,1)S(1)}, bf16[2,128,512]{2,1,0:T(8,128)(2,1)S(1)}, u32[]{:S(2)}, u32[]{:S(2)}) collective-permute-start(bf16[2,128,512]{2,1,0:T(8,128)(2,1)S(1)} %pad_maximum_fusion.1.first), channel_id=1, source_target_pairs={{0,192},{1,577},{192,384},{193,1},{384,576},{385,193},{576,0},{577... | collective-permute-start | bytes 786440 | tf_op jit(solution)/shard_map/ppermute | solution.py:149
  58.9 12.6 %collective-permute-start.4 = (bf16[768,512]{1,0:T(8,128)(2,1)S(1)}, bf16[768,512]{1,0:T(8,128)(2,1)S(1)}, u32[]{:S(2)}, u32[]{:S(2)}) collective-permute-start(bf16[768,512]{1,0:T(8,128)(2,1)S(1)} %bitcast.26), channel_id=1, source_target_pairs={{0,1},{1,0},{2,3},{3,2},{4,5},{5,4},{6,7},{7,6},{8,9},{9,8},{10,11... | collective-permute-start | bytes 2359304 | tf_op jit(solution)/shard_map/ppermute | solution.py:191
  73.3 22.5 %all-to-all-start.1 = ((bf16[6,128,512]{2,1,0:T(8,128)(2,1)}), bf16[6,128,512]{2,1,0:T(8,128)(2,1)}, u32[]{:S(2)}, u32[]{:S(2)}) async-start(bf16[6,128,512]{2,1,0:T(8,128)(2,1)} %bitcast.14), calls=%async_computation.1 | async-start | bytes 1572864 | tf_op jit(solution)/shard_map/all_to_all | solution.py:215
  84.4 21.4 %collective-permute-start.6 = (bf16[2,256,1536]{2,1,0:T(8,128)(2,1)}, bf16[2,256,1536]{2,1,0:T(8,128)(2,1)S(1)}, u32[]{:S(2)}, u32[]{:S(2)}) collective-permute-start(bf16[2,256,1536]{2,1,0:T(8,128)(2,1)} %pad_maximum_fusion), channel_id=1, source_target_pairs={{0,1},{1,0},{2,3},{3,2},{4,5},{5,4},{6,7},{7,6},{8,9},{9,8},{10,11... | collective-permute-start | bytes 4718600 | tf_op jit(solution)/shard_map/ppermute | solution.py:198
